TPU v7x, 32 devices: a whole 2x2x4 slice. The times are simulated.
32 devices in a mesh: dp: 4 (over y, x), row: 4 (over z), col: 2 (over core).
Axes of the slice: x: 2, y: 2, z: 4, core: 2. Of those that a mesh axis runs over, the one named last changes fastest.
Arguments:
- tokens_in: bfloat16 [6144, 768], P(('dp', 'row', 'col')), may hold values from -6 to 6
- lengths: int32 [16], P(('dp', 'row')), may hold values from 192 to 384, as said below
- cotangent: bfloat16 [6144, 768], P(('dp', 'row', 'col')), may hold values from -6 to 6
- norm_gain: float32 [2, 768], replicated, may hold values from 0.5 to 1.5
- norm_shift: float32 [2, 768], replicated, may hold values from -1.75 to 1.75
- w_fwd: float32 [2, 768, 1536], P(None, 'row', 'col'), may hold values from -0.21875 to 0.21875
- w_bwd: float32 [2, 768, 1536], P(None, 'row', 'col'), may hold values from -0.21875 to 0.21875
- w_value: float32 [2, 768, 3072], P(None, 'row', 'col'), may hold values from -0.21875 to 0.21875
- bias_fwd: float32 [2, 1536], P(None, 'col'), may hold values from -1.75 to 1.75
- bias_bwd: float32 [2, 1536], P(None, 'col'), may hold values from -1.75 to 1.75
- bias_value: float32 [2, 3072], P(None, 'col'), may hold values from -1.75 to 1.75
- decay_log: float32 [2, 2, 1536, 64], P(None, None, 'col'), may hold values from -2 to 3
- step_log: float32 [2, 2, 1536], P(None, None, 'col'), may hold values from -6.9 to -2.3
- b_input: float32 [2, 2, 1536, 64], P(None, None, 'col'), may hold values from -6 to 6
- c_output: float32 [2, 2, 1536, 64], P(None, None, 'col'), may hold values from -0.75 to 0.75
- skip_gain: float32 [2, 2, 1536], P(None, None, 'col'), may hold values from -6 to 6
- w_mix: float32 [2, 1536, 3072], P(None, 'row', 'col'), may hold values from -0.15625 to 0.15625
- bias_mix: float32 [2, 3072], P(None, 'col'), may hold values from -1.75 to 1.75
- w_output: float32 [2, 3072, 768], P(None, 'col', 'row'), may hold values from -0.4375 to 0.4375
- bias_output: float32 [2, 768], replicated, may hold values from -1.75 to 1.75
Outputs:
- tokens_out: bfloat16 [6144, 768], P(('dp', 'row', 'col'))
- grad_tokens: float32 [6144, 768], P(('dp', 'row', 'col'))
- grad_norm_gain: float32 [2, 768], replicated
- grad_norm_shift: float32 [2, 768], replicated
- grad_w_fwd: float32 [2, 768, 1536], P(None, 'row', 'col')
- grad_w_bwd: float32 [2, 768, 1536], P(None, 'row', 'col')
- grad_w_value: float32 [2, 768, 3072], P(None, 'row', 'col')
- grad_bias_fwd: float32 [2, 1536], P(None, 'col')
- grad_bias_bwd: float32 [2, 1536], P(None, 'col')
- grad_bias_value: float32 [2, 3072], P(None, 'col')
- grad_decay_log: float32 [2, 2, 1536, 64], P(None, None, 'col')
- grad_step_log: float32 [2, 2, 1536], P(None, None, 'col')
- grad_b_input: float32 [2, 2, 1536, 64], P(None, None, 'col')
- grad_c_output: float32 [2, 2, 1536, 64], P(None, None, 'col')
- grad_skip_gain: float32 [2, 2, 1536], P(None, None, 'col')
- grad_w_mix: float32 [2, 1536, 3072], P(None, 'row', 'col')
- grad_bias_mix: float32 [2, 3072], P(None, 'col')
- grad_w_output: float32 [2, 3072, 768], P(None, 'col', 'row')
- grad_bias_output: float32 [2, 768], replicated
Inputs may be any that keep to these rules, and one draw needn't show every extreme that they name: `lengths`: each slot's sequence starts at the slot's first position and the rest of the slot is padding; some slot is full and some holds exactly 192 tokens.
All inputs are finite; a program needn't handle non-finite values.
Results may differ from a plain program's by a relative error of at most 0.025.
Values may be sent and summed in bfloat16 or wider, within the bound.
A program may use at most 448 MiB of HBM per device.

v0:
```python
import jax
import jax.numpy as jnp
from jax import lax
from jax.sharding import PartitionSpec as P

LAYERS = 2
QB = 64


HIGH = lax.Precision.HIGHEST
EPS = 1e-05


def norm_rows(residual, gain_now, shift_now):
    row_mean = jnp.mean(residual, axis=1, keepdims=True)
    centered = residual - row_mean
    variance = jnp.mean(centered * centered, axis=1, keepdims=True)
    return centered * lax.rsqrt(variance + EPS) * gain_now + shift_now


def ssm_scan(signal, decay_now, step_now, b_now, c_now, skip_now):
    length_rows, channels = signal.shape
    blocks_count = length_rows // QB
    decay_rate = jnp.exp(step_now)[:, None] * jnp.exp(decay_now)
    b_disc = (1.0 - jnp.exp(-decay_rate)) * jnp.exp(-decay_now) * b_now
    offsets = jnp.arange(QB, dtype=jnp.float32)
    lag_int = jnp.arange(QB, dtype=jnp.int32)
    lag_index = jnp.clip(lag_int[:, None] - lag_int[None, :], 0, QB - 1)
    causal = lag_int[:, None] >= lag_int[None, :]
    powers = jnp.exp(-offsets[:, None, None] * decay_rate[None])
    kernel = jnp.sum(powers * (c_now * b_disc)[None], axis=2)
    toeplitz = jnp.where(causal[:, :, None], jnp.take(kernel, lag_index, axis=0), 0.0)
    blocks = signal.reshape(blocks_count, QB, channels)
    inside = jnp.einsum("tsc,bsc->btc", toeplitz, blocks, precision=HIGH)
    tail = jnp.exp(-(QB - 1.0 - offsets)[:, None, None] * decay_rate[None]) * b_disc[None]
    block_ends = jnp.einsum("bsc,scn->bcn", blocks, tail, precision=HIGH)
    block_decay = jnp.exp(-QB * decay_rate)

    def advance(carry_state, block_end):
        return (block_decay * carry_state + block_end, carry_state)

    unused_state, block_starts = lax.scan(advance, jnp.zeros_like(decay_rate), block_ends)
    head = jnp.exp(-(offsets + 1.0)[:, None, None] * decay_rate[None]) * c_now[None]
    carried = jnp.einsum("bcn,tcn->btc", block_starts, head, precision=HIGH)
    return (inside + carried).reshape(length_rows, channels) + skip_now * signal


def both_scans(fwd_in, bwd_in, ssm_params):
    decay_now, step_now, b_now, c_now, skip_now = ssm_params
    fwd_out = ssm_scan(fwd_in, decay_now[0], step_now[0], b_now[0], c_now[0], skip_now[0])
    bwd_out = ssm_scan(bwd_in[::-1], decay_now[1], step_now[1], b_now[1], c_now[1], skip_now[1])[
        ::-1
    ]
    return (fwd_out, bwd_out)


def input_acts(pre_all, live_mask, chan_cols):
    fwd_in = jax.nn.gelu(pre_all[:, :chan_cols]) * live_mask[:, None]
    bwd_in = jax.nn.gelu(pre_all[:, chan_cols : 2 * chan_cols]) * live_mask[:, None]
    value_act = jax.nn.gelu(pre_all[:, 2 * chan_cols :])
    return (fwd_in, bwd_in, value_act)


def cross_rows(left, right):
    return lax.dot_general(
        left, right, (((0,), (0,)), ((), ())), preferred_element_type=jnp.float32
    )


def times_turned(left, right):
    return lax.dot_general(
        left, right, (((1,), (1,)), ((), ())), preferred_element_type=jnp.float32
    )


def body(
    tokens_in,
    lengths,
    cotangent,
    norm_gain,
    norm_shift,
    w_fwd,
    w_bwd,
    w_value,
    bias_fwd,
    bias_bwd,
    bias_value,
    decay_log,
    step_log,
    b_input,
    c_output,
    skip_gain,
    w_mix,
    bias_mix,
    w_output,
    bias_output,
):
    tok_rows = tokens_in.shape[0]
    slot_rows = tok_rows * lax.axis_size("col")
    chan_cols = w_fwd.shape[2]
    positions = jnp.arange(slot_rows, dtype=jnp.int32)
    live_mask = (positions < lengths[0]).astype(jnp.float32)
    own_mask = lax.dynamic_slice_in_dim(live_mask, lax.axis_index("col") * tok_rows, tok_rows, 0)
    residual = tokens_in.astype(jnp.float32)
    stored = []
    for depth_index in range(LAYERS):
        normed_low = norm_rows(residual, norm_gain[depth_index], norm_shift[depth_index]).astype(
            jnp.bfloat16
        )
        in_parts = (
            lax.all_gather(w_fwd[depth_index].astype(jnp.bfloat16), "row", axis=0, tiled=True),
            lax.all_gather(w_bwd[depth_index].astype(jnp.bfloat16), "row", axis=0, tiled=True),
            lax.all_gather(w_value[depth_index].astype(jnp.bfloat16), "row", axis=0, tiled=True),
        )
        in_matrix = jnp.concatenate(in_parts, axis=1)
        gathered = lax.all_gather(normed_low, "col", axis=0, tiled=True)
        in_bias = jnp.concatenate(
            (bias_fwd[depth_index], bias_bwd[depth_index], bias_value[depth_index])
        )
        pre_all = jnp.dot(gathered, in_matrix, preferred_element_type=jnp.float32) + in_bias
        fwd_in, bwd_in, value_act = input_acts(pre_all, live_mask, chan_cols)
        ssm_params = (
            decay_log[depth_index],
            step_log[depth_index],
            b_input[depth_index],
            c_output[depth_index],
            skip_gain[depth_index],
        )
        fwd_out, bwd_out = both_scans(fwd_in, bwd_in, ssm_params)
        mixed_low = (fwd_out * bwd_out).astype(jnp.bfloat16)
        mix_full = lax.all_gather(mixed_low, "col", axis=1, tiled=True)
        mix_matrix, out_matrix = (
            lax.all_gather(w_mix[depth_index].astype(jnp.bfloat16), "row", axis=0, tiled=True),
            lax.all_gather(w_output[depth_index].astype(jnp.bfloat16), "row", axis=1, tiled=True),
        )
        pre_mix = (
            jnp.dot(mix_full, mix_matrix, preferred_element_type=jnp.float32)
            + bias_mix[depth_index]
        )
        product_low = (jax.nn.gelu(pre_mix) * value_act).astype(jnp.bfloat16)
        branch = lax.psum_scatter(
            jnp.dot(product_low, out_matrix, preferred_element_type=jnp.float32).astype(
                jnp.bfloat16
            ),
            "col",
            scatter_dimension=0,
            tiled=True,
        ).astype(jnp.float32)
        stored.append(
            (
                residual,
                normed_low,
                gathered,
                pre_all,
                ssm_params,
                mixed_low,
                mix_full,
                in_matrix,
                mix_matrix,
                out_matrix,
                pre_mix,
                product_low,
            )
        )
        residual = residual + own_mask[:, None] * (branch + bias_output[depth_index])
    tokens_out = residual.astype(jnp.bfloat16)
    grad = cotangent.astype(jnp.float32)
    layer_grads = []
    for depth_index in reversed(range(LAYERS)):
        (
            resid_in,
            normed_low,
            gathered,
            pre_all,
            ssm_params,
            mixed_low,
            mix_full,
            in_matrix,
            mix_matrix,
            out_matrix,
            pre_mix,
            product_low,
        ) = stored[depth_index]
        fwd_in, bwd_in, value_act = input_acts(pre_all, live_mask, chan_cols)
        grad_branch = grad * own_mask[:, None]
        grad_out_full = lax.all_gather(grad_branch.astype(jnp.bfloat16), "col", axis=0, tiled=True)
        grad_product = times_turned(grad_out_full, out_matrix)
        grad_w_output = cross_rows(product_low, grad_out_full)
        gated, gelu_pull = jax.vjp(jax.nn.gelu, pre_mix)
        grad_value = grad_product * gated
        grad_pre_mix = gelu_pull(grad_product * value_act)[0]
        grad_mix_low = grad_pre_mix.astype(jnp.bfloat16)
        grad_mixed = lax.psum_scatter(
            times_turned(grad_mix_low, mix_matrix).astype(jnp.bfloat16),
            "col",
            scatter_dimension=1,
            tiled=True,
        ).astype(jnp.float32)
        grad_w_mix = cross_rows(mix_full, grad_mix_low)
        scan_outs, scan_pull = jax.vjp(both_scans, fwd_in, bwd_in, ssm_params)
        fwd_out, bwd_out = scan_outs
        grad_fwd_in, grad_bwd_in, grad_ssm = scan_pull((grad_mixed * bwd_out, grad_mixed * fwd_out))
        unused_acts, act_pull = jax.vjp(
            lambda pre_values: input_acts(pre_values, live_mask, chan_cols), pre_all
        )
        grad_pre_all = act_pull((grad_fwd_in, grad_bwd_in, grad_value))[0]
        grad_pre_low = grad_pre_all.astype(jnp.bfloat16)
        grad_normed = lax.psum_scatter(
            times_turned(grad_pre_low, in_matrix).astype(jnp.bfloat16),
            "col",
            scatter_dimension=0,
            tiled=True,
        ).astype(jnp.float32)
        grad_w_in = cross_rows(gathered, grad_pre_low)
        unused_norm, norm_pull = jax.vjp(
            norm_rows, resid_in, norm_gain[depth_index], norm_shift[depth_index]
        )
        grad_resid, grad_gain, grad_shift = norm_pull(grad_normed)
        row_in, row_mix, row_out = (
            lax.psum_scatter(
                grad_w_in.astype(jnp.bfloat16), "row", scatter_dimension=0, tiled=True
            ).astype(jnp.float32),
            lax.psum_scatter(
                grad_w_mix.astype(jnp.bfloat16), "row", scatter_dimension=0, tiled=True
            ).astype(jnp.float32),
            lax.psum_scatter(
                grad_w_output.astype(jnp.bfloat16), "row", scatter_dimension=1, tiled=True
            ).astype(jnp.float32),
        )
        sum_in, sum_mix, sum_out = (
            lax.psum(row_in.astype(jnp.bfloat16), "dp").astype(jnp.float32),
            lax.psum(row_mix.astype(jnp.bfloat16), "dp").astype(jnp.float32),
            lax.psum(row_out.astype(jnp.bfloat16), "dp").astype(jnp.float32),
        )
        chan_sums = lax.psum(
            (
                jnp.sum(grad_pre_all, axis=0),
                jnp.sum(grad_pre_mix, axis=0),
                grad_ssm[0],
                grad_ssm[1],
                grad_ssm[2],
                grad_ssm[3],
                grad_ssm[4],
            ),
            ("dp", "row"),
        )
        norm_sums = lax.psum(
            (grad_gain, grad_shift, jnp.sum(grad_branch, axis=0)), ("dp", "row", "col")
        )
        bias_sums = chan_sums[0]
        layer_grads.append(
            (
                norm_sums[0],
                norm_sums[1],
                sum_in[:, :chan_cols],
                sum_in[:, chan_cols : 2 * chan_cols],
                sum_in[:, 2 * chan_cols :],
                bias_sums[:chan_cols],
                bias_sums[chan_cols : 2 * chan_cols],
                bias_sums[2 * chan_cols :],
                chan_sums[2],
                chan_sums[3],
                chan_sums[4],
                chan_sums[5],
                chan_sums[6],
                sum_mix,
                chan_sums[1],
                sum_out,
                norm_sums[2],
            )
        )
        grad = grad + grad_resid
    ordered = layer_grads[::-1]
    stacked = [jnp.stack([entry[position] for entry in ordered]) for position in range(17)]
    return (
        tokens_out,
        grad,
        stacked[0],
        stacked[1],
        stacked[2],
        stacked[3],
        stacked[4],
        stacked[5],
        stacked[6],
        stacked[7],
        stacked[8],
        stacked[9],
        stacked[10],
        stacked[11],
        stacked[12],
        stacked[13],
        stacked[14],
        stacked[15],
        stacked[16],
    )


def solution(mesh):
    in_specs = (
        P(("dp", "row", "col"), None),
        P(("dp", "row")),
        P(("dp", "row", "col"), None),
        P(),
        P(),
        P(None, "row", "col"),
        P(None, "row", "col"),
        P(None, "row", "col"),
        P(None, "col"),
        P(None, "col"),
        P(None, "col"),
        P(None, None, "col", None),
        P(None, None, "col"),
        P(None, None, "col", None),
        P(None, None, "col", None),
        P(None, None, "col"),
        P(None, "row", "col"),
        P(None, "col"),
        P(None, "col", "row"),
        P(),
    )
    out_specs = (
        P(("dp", "row", "col"), None),
        P(("dp", "row", "col"), None),
        P(),
        P(),
        P(None, "row", "col"),
        P(None, "row", "col"),
        P(None, "row", "col"),
        P(None, "col"),
        P(None, "col"),
        P(None, "col"),
        P(None, None, "col", None),
        P(None, None, "col"),
        P(None, None, "col", None),
        P(None, None, "col", None),
        P(None, None, "col"),
        P(None, "row", "col"),
        P(None, "col"),
        P(None, "col", "row"),
        P(),
    )
    return jax.shard_map(body, mesh=mesh, in_specs=in_specs, out_specs=out_specs, check_vma=False)
```

profile of v0, /device:TPU:0, one launch (start us, length us, event | category | flops | bytes accessed | tf_op | source)
XLA Modules:
  0.0 3022.4 jit_solution(15727393071781162672)
XLA Ops:
  26.5 30.8 %multiply_reduce_fusion.9 = (f32[64,768]{0,1:T(8,128)}, f32[64,768]{0,1:T(8,128)S(1)}, f32[64,768]{0,1:T(8,128)}, f32[64,768]{0,1:T(8,128)S(1)}) fusion(f32[768,64]{1,0:T(8,128)} %get-tuple-element.1415, f32[768,64]{1,0:T(8,128)} %get-tuple-element.1413, f32[64]{0:T(128)S(1)} %copy-done.253, f32[768,64]{1,0:T(8,128)} %get-tuple-element.1326, ...), kind=kLoop, calls=%fused_computation.126 | loop fusion | flops 37552128 | bytes 2359552 | tf_op jit(solution)/shard_map/reduce_sum | solution.py:31
  76.3 23.4 copy.261
  117.8 23.5 copy.251
  166.0 28.0 fusion.283
  195.5 33.1 %while.149 = (s32[]{:T(128)}, f32[768,64]{1,0:T(8,128)}, f32[6,768,64]{2,1,0:T(8,128)}, f32[768,64]{1,0:T(8,128)S(1)}, f32[6,768,64]{2,0,1:T(8,128)}, /*index=5*/s32[]{:T(128)}, s32[]{:T(128)}) while((s32[]{:T(128)}, f32[768,64]{1,0:T(8,128)}, f32[6,768,64]{2,1,0:T(8,128)}, f32[768,64]{1,0:T(8,128)S(1)}, f32[6,768,64]{2,0,1:T(8,128)}, ...), condition=%wide.region_7.9_spmd.clone, body=%wide.region_6.8_spmd.clone.sunk | while | flops 196611 | bytes 1966184 | solution.py:42
  228.7 42.5 %fusion.79 = f32[768,6,64]{2,1,0:T(8,128)S(1)} fusion(f32[6,64,768]{1,0,2:T(8,128)S(1)} %copy.262, f32[64,64,768]{1,0,2:T(8,128)} %copy.261, pred[64,64]{1,0:T(8,128)(4,1)S(1)} %get-tuple-element.1422, pred[64,64]{1,0:T(8,128)(4,1)S(1)} %get-tuple-element.1421), kind=kOutput, calls=%fused_computation.151 | convolution fusion | flops 232783872 | bytes 14950400 | tf_op jit(solution)/shard_map/tsc,bsc->btc/dot_general | solution.py:34
  271.2 44.5 %bitcast_add_fusion.2 = f32[6,64,768]{1,0,2:T(8,128)} fusion(f32[768,6,64]{2,1,0:T(8,128)S(1)} %fusion.79, f32[6,768,64]{2,1,0:T(8,128)S(1)} %copy-done.30, f32[768,64]{1,0:T(8,128)S(1)} %bitcast.873, f32[768,64]{1,0:T(8,128)S(1)} %copy-done.168, f32[64]{0:T(128)S(1)} %copy-done.248), kind=kOutput, calls=%fused_computation.310 | convolution fusion | flops 233078784 | bytes 3932416 | tf_op jit(solution)/shard_map/bcn,tcn->btc/dot_general | solution.py:44
  327.1 44.4 %fusion.77 = f32[768,6,64]{2,1,0:T(8,128)} fusion(f32[6,64,768]{1,0,2:T(8,128)S(1)} %copy.252, f32[64,64,768]{1,0,2:T(8,128)} %copy.251, pred[64,64]{1,0:T(8,128)(4,1)S(1)} %get-tuple-element.1422, pred[64,64]{1,0:T(8,128)(4,1)S(1)} %get-tuple-element.1421), kind=kOutput, calls=%fused_computation.149 | convolution fusion | flops 232783872 | bytes 14950400 | tf_op jit(solution)/shard_map/tsc,bsc->btc/dot_general | solution.py:34
  371.6 26.2 fusion.271
  398.0 28.8 while.148
  426.8 46.2 %bitcast_add_fusion.3 = f32[6,64,768]{1,0,2:T(8,128)} fusion(f32[768,6,64]{2,1,0:T(8,128)} %fusion.77, f32[6,768,64]{2,1,0:T(8,128)S(1)} %get-tuple-element.1922, f32[768,64]{1,0:T(8,128)S(1)} %bitcast.877, f32[64]{0:T(128)} %get-tuple-element.1424, f32[768,64]{1,0:T(8,128)S(1)} %copy-done.160), kind=kOutput, calls=%fused_computation.311 | convolution fusion | flops 233078784 | bytes 3932416 | tf_op jit(solution)/shard_map/bcn,tcn->btc/dot_general | solution.py:44
  490.9 92.6 %all-gather.33.cloned.1.call-done = bf16[1,1536,1536]{2,1,0:T(8,128)(2,1)} async-done(((bf16[1,384,1536]{2,1,0:T(8,128)(2,1)}), bf16[1,1536,1536]{2,1,0:T(8,128)(2,1)}) %all-gather.33.cloned.1.call-update) | async-done | bytes 4718608 | tf_op jit(solution)/shard_map/all_gather | solution.py:133
  591.4 43.1 %all-gather.35.cloned.1.call-done = bf16[1,1536,768]{1,2,0:T(8,128)(2,1)} async-done(((bf16[1,1536,192]{1,2,0:T(8,128)(2,1)}), bf16[1,1536,768]{1,2,0:T(8,128)(2,1)}) %all-gather.35.cloned.1.call-update) | async-done | bytes 2359312 | tf_op jit(solution)/shard_map/all_gather | solution.py:134
  660.5 23.5 copy.281
  702.2 23.5 copy.271
  732.9 29.0 all-gather.41.cloned.1.call-done
  778.4 44.4 %fusion.83 = f32[768,6,64]{2,1,0:T(8,128)} fusion(f32[6,64,768]{1,0,2:T(8,128)S(1)} %copy.282, f32[64,64,768]{1,0,2:T(8,128)} %copy.281, pred[64,64]{1,0:T(8,128)(4,1)S(1)} %get-tuple-element.1422, pred[64,64]{1,0:T(8,128)(4,1)S(1)} %get-tuple-element.1421), kind=kOutput, calls=%fused_computation.155 | convolution fusion | flops 232783872 | bytes 14950400 | tf_op jit(solution)/shard_map/tsc,bsc->btc/dot_general | solution.py:34
  822.8 26.5 fusion.307
  850.9 33.5 %while.151 = (s32[]{:T(128)}, f32[768,64]{1,0:T(8,128)}, f32[6,768,64]{2,1,0:T(8,128)}, f32[768,64]{1,0:T(8,128)S(1)}, f32[6,768,64]{2,0,1:T(8,128)}, /*index=5*/s32[]{:T(128)}, s32[]{:T(128)}) while((s32[]{:T(128)}, f32[768,64]{1,0:T(8,128)}, f32[6,768,64]{2,1,0:T(8,128)}, f32[768,64]{1,0:T(8,128)S(1)}, ...), condition=%wide.region_16.18_spmd.clone, body=%wide.region_15.17_spmd.clone.sunk | while | flops 196611 | bytes 1966184 | solution.py:42
  884.3 45.7 %bitcast_add_fusion = f32[6,64,768]{1,0,2:T(8,128)} fusion(f32[768,6,64]{2,1,0:T(8,128)S(1)} %copy-done.66, f32[6,768,64]{2,1,0:T(8,128)} %get-tuple-element.1832, f32[768,64]{1,0:T(8,128)} %bitcast.879, f32[768,64]{1,0:T(8,128)} %copy-done.154, f32[64]{0:T(128)} %get-tuple-element.1424), kind=kOutput, calls=%fused_computation.308 | convolution fusion | flops 233078784 | bytes 3932416 | tf_op jit(solution)/shard_map/bcn,tcn->btc/dot_general | solution.py:44
  941.5 27.3 fusion.295
  968.8 43.3 %fusion.81 = f32[768,6,64]{2,1,0:T(8,128)} fusion(f32[6,64,768]{1,0,2:T(8,128)S(1)} %copy.272, f32[64,64,768]{1,0,2:T(8,128)} %copy.271, pred[64,64]{1,0:T(8,128)(4,1)S(1)} %get-tuple-element.1422, pred[64,64]{1,0:T(8,128)(4,1)S(1)} %get-tuple-element.1421), kind=kOutput, calls=%fused_computation.153 | convolution fusion | flops 232783872 | bytes 14950400 | tf_op jit(solution)/shard_map/tsc,bsc->btc/dot_general | solution.py:34
  1013.7 33.7 %while.150 = (s32[]{:T(128)}, f32[768,64]{1,0:T(8,128)}, f32[6,768,64]{2,1,0:T(8,128)}, f32[768,64]{1,0:T(8,128)S(1)}, f32[6,768,64]{2,0,1:T(8,128)}, /*index=5*/s32[]{:T(128)}, s32[]{:T(128)}) while((s32[]{:T(128)}, f32[768,64]{1,0:T(8,128)}, f32[6,768,64]{2,1,0:T(8,128)}, f32[768,64]{1,0:T(8,128)S(1)}, ...), condition=%wide.region_13.15_spmd.clone, body=%wide.region_12.14_spmd.clone.sunk | while | flops 196611 | bytes 1966184 | solution.py:42
  1047.3 45.7 %bitcast_add_fusion.1 = f32[6,64,768]{1,0,2:T(8,128)} fusion(f32[768,6,64]{2,1,0:T(8,128)S(1)} %copy-done.67, f32[6,768,64]{2,1,0:T(8,128)} %get-tuple-element.1862, f32[768,64]{1,0:T(8,128)} %bitcast.882, f32[768,64]{1,0:T(8,128)} %get-tuple-element.1413, f32[64]{0:T(128)} %get-tuple-element.1424), kind=kOutput, calls=%fused_computation.309 | convolution fusion | flops 233078784 | bytes 3932416 | tf_op jit(solution)/shard_map/bcn,tcn->btc/dot_general | solution.py:44
  1147.5 26.0 fusion.82
  1173.5 24.4 fusion.302
  1200.2 26.0 fusion.80
  1226.2 24.1 fusion.290
  1250.5 32.6 %while.152 = (s32[]{:T(128)}, f32[768,64]{1,0:T(8,128)}, f32[768,64]{1,0:T(8,128)}, f32[6,768,64]{2,1,0:T(8,128)S(1)}, f32[6,768,64]{2,1,0:T(8,128)}, /*index=5*...) while((s32[]{:T(128)}, f32[768,64]{1,0:T(8,128)}, ...), condition=%wide.region_20.23_spmd.clone, body=%wide.region_19.22_spmd.clone.sunk | while | flops 344068 | bytes 2359440 | solution.py:42
  1284.5 43.4 %add_bitcast_fusion.3 = f32[6,64,768]{1,0,2:T(8,128)} fusion(f32[768,6,64]{2,1,0:T(8,128)} %fusion.82, f32[768,64]{1,0:T(8,128)S(1)} %copy-done.153, f32[768,64]{1,0:T(8,128)S(1)} %copy-done.157, f32[64]{0:T(128)} %get-tuple-element.1423, f32[768,64,6]{1,0,2:T(8,128)S(1)} %bitcast.857), kind=kOutput, calls=%fused_computation.315 | convolution fusion | flops 233078784 | bytes 3932416 | tf_op jit(solution)/shard_map/transpose(jvp(bsc,scn->bcn))/dot_general | solution.py:36
  1344.3 26.2 while.153
  1370.5 44.4 %add_bitcast_fusion.2 = f32[6,64,768]{1,0,2:T(8,128)} fusion(f32[768,6,64]{2,1,0:T(8,128)} %fusion.80, f32[768,64]{1,0:T(8,128)} %get-tuple-element.1416, f32[768,64]{1,0:T(8,128)} %get-tuple-element.1413, f32[64]{0:T(128)} %get-tuple-element.1423, f32[768,64,6]{1,0,2:T(8,128)S(1)} %bitcast.859), kind=kOutput, calls=%fused_computation.314 | convolution fusion | flops 233078784 | bytes 3932416 | tf_op jit(solution)/shard_map/transpose(jvp(bsc,scn->bcn))/dot_general | solution.py:36
  1492.9 43.6 %select_bitcast_fusion = f32[64,64,768]{1,0,2:T(8,128)} fusion(pred[64,64]{1,0:T(8,128)(4,1)S(1)} %get-tuple-element.1421, f32[6,64,768]{1,0,2:T(8,128)S(1)} %copy-done.8, f32[6,64,768]{1,0,2:T(8,128)} %copy-done.17), kind=kOutput, calls=%fused_computation.98 | convolution fusion | flops 229638144 | bytes 14946304 | tf_op jit(solution)/shard_map/transpose(jvp(tsc,bsc->btc))/dot_general | solution.py:34
  1536.6 21.1 copy.344
  1557.7 28.6 scatter_custom_fusion.3
  1609.1 26.0 fusion.78
  1635.2 24.1 fusion.278
  1659.5 32.3 %while.154 = (s32[]{:T(128)}, f32[768,64]{1,0:T(8,128)}, f32[768,64]{1,0:T(8,128)}, f32[6,768,64]{2,1,0:T(8,128)S(1)}, f32[6,768,64]{2,1,0:T(8,128)}, /*index=5*...) while((s32[]{:T(128)}, f32[768,64]{1,0:T(8,128)}, ...), condition=%wide.region_28.31_spmd.clone, body=%wide.region_27.30_spmd.clone.sunk | while | flops 344068 | bytes 2359440 | solution.py:42
  1693.2 43.5 %add_bitcast_fusion.1 = f32[6,64,768]{1,0,2:T(8,128)} fusion(f32[768,6,64]{2,1,0:T(8,128)} %fusion.78, f32[768,64]{1,0:T(8,128)S(1)} %copy-done.167, f32[768,64]{1,0:T(8,128)S(1)} %copy-done.170, f32[64]{0:T(128)} %get-tuple-element.1423, f32[768,64,6]{1,0,2:T(8,128)S(1)} %bitcast.861), kind=kOutput, calls=%fused_computation.313 | convolution fusion | flops 233078784 | bytes 3932416 | tf_op jit(solution)/shard_map/transpose(jvp(bsc,scn->bcn))/dot_general | solution.py:36
  1753.9 25.1 fusion.266
  1779.0 25.0 fusion.76
  1804.2 32.1 %while.155 = (s32[]{:T(128)}, f32[768,64]{1,0:T(8,128)}, f32[768,64]{1,0:T(8,128)}, f32[6,768,64]{2,1,0:T(8,128)S(1)}, f32[6,768,64]{2,1,0:T(8,128)}, /*index=5*...) while((s32[]{:T(128)}, f32[768,64]{1,0:T(8,128)}, ...), condition=%wide.region_30.33_spmd.clone, body=%wide.region_29.32_spmd.clone.sunk | while | flops 344068 | bytes 2359440 | solution.py:42
  1836.3 44.0 %add_bitcast_fusion = f32[6,64,768]{1,0,2:T(8,128)} fusion(f32[768,6,64]{2,1,0:T(8,128)} %fusion.76, f32[768,64]{1,0:T(8,128)S(1)} %copy-done.164, f32[64]{0:T(128)S(1)} %copy-done.246, f32[768,64]{1,0:T(8,128)S(1)} %copy-done.161, f32[768,64,6]{1,0,2:T(8,128)S(1)} %bitcast.863), kind=kOutput, calls=%fused_computation.312 | convolution fusion | flops 233078784 | bytes 3932416 | tf_op jit(solution)/shard_map/transpose(jvp(bsc,scn->bcn))/dot_general | solution.py:36
  1895.4 43.6 %select_bitcast_fusion.1 = f32[64,64,768]{1,0,2:T(8,128)} fusion(pred[64,64]{1,0:T(8,128)(4,1)S(1)} %get-tuple-element.1421, f32[6,64,768]{1,0,2:T(8,128)S(1)} %copy-done.5, f32[6,64,768]{1,0,2:T(8,128)} %copy-done.15), kind=kOutput, calls=%fused_computation.101 | convolution fusion | flops 229638144 | bytes 14946304 | tf_op jit(solution)/shard_map/transpose(jvp(tsc,bsc->btc))/dot_general | solution.py:34
  1939.1 20.8 copy.338
  1959.9 28.7 scatter_custom_fusion.2
  1989.5 43.7 %fusion.178 = f32[768,64,64]{1,2,0:T(8,128)} fusion(f32[6,64,768]{1,0,2:T(8,128)S(1)} %copy-done.9, f32[768,64,6]{1,0,2:T(8,128)} %bitcast.860), kind=kOutput, calls=%fused_computation.270 | convolution fusion | flops 226492416 | bytes 14942208 | tf_op jit(solution)/shard_map/transpose(jvp(bsc,scn->bcn))/dot_general | solution.py:36
  2033.3 42.7 %fusion.181 = f32[768,64,64]{1,2,0:T(8,128)} fusion(f32[6,64,768]{1,0,2:T(8,128)S(1)} %copy-done.6, f32[768,64,6]{1,0,2:T(8,128)S(1)} %bitcast.858), kind=kOutput, calls=%fused_computation.273 | convolution fusion | flops 226492416 | bytes 14942208 | tf_op jit(solution)/shard_map/transpose(jvp(bsc,scn->bcn))/dot_general | solution.py:36
  2076.0 42.7 %select_bitcast_fusion.3 = f32[64,64,768]{1,0,2:T(8,128)} fusion(pred[64,64]{1,0:T(8,128)(4,1)S(1)} %get-tuple-element.1421, f32[6,64,768]{1,0,2:T(8,128)S(1)} %copy-done.1, f32[6,64,768]{1,0,2:T(8,128)S(1)} %copy-done.11), kind=kOutput, calls=%fused_computation.107 | convolution fusion | flops 229638144 | bytes 14946304 | tf_op jit(solution)/shard_map/transpose(jvp(tsc,bsc->btc))/dot_general | solution.py:34
  2118.6 20.5 copy.326
  2139.2 28.2 scatter_custom_fusion
  2168.4 44.3 %select_bitcast_fusion.2 = f32[64,64,768]{1,0,2:T(8,128)} fusion(pred[64,64]{1,0:T(8,128)(4,1)S(1)} %get-tuple-element.1421, f32[6,64,768]{1,0,2:T(8,128)} %copy-done.2, f32[6,64,768]{1,0,2:T(8,128)} %copy-done.13), kind=kOutput, calls=%fused_computation.104 | convolution fusion | flops 229638144 | bytes 14946304 | tf_op jit(solution)/shard_map/transpose(jvp(tsc,bsc->btc))/dot_general | solution.py:34
  2212.7 20.5 copy.332
  2233.2 28.4 scatter_custom_fusion.1
  2269.2 43.8 %fusion.175 = f32[768,64,64]{1,2,0:T(8,128)} fusion(f32[6,64,768]{1,0,2:T(8,128)S(1)} %copy-done.1, f32[768,64,6]{1,0,2:T(8,128)} %bitcast.862), kind=kOutput, calls=%fused_computation.267 | convolution fusion | flops 226492416 | bytes 14942208 | tf_op jit(solution)/shard_map/transpose(jvp(bsc,scn->bcn))/dot_general | solution.py:36
  2313.0 42.7 %fusion.190 = f32[768,64,64]{2,1,0:T(8,128)} fusion(f32[6,768,64]{2,1,0:T(8,128)S(1)} %copy-done.31, f32[6,64,768]{1,0,2:T(8,128)S(1)} %copy-done.12), kind=kOutput, calls=%fused_computation.282 | convolution fusion | flops 226492416 | bytes 14942208 | tf_op jit(solution)/shard_map/transpose(jvp(bcn,tcn->btc))/dot_general | solution.py:44
  2355.7 42.9 %fusion.172 = f32[768,64,64]{1,2,0:T(8,128)} fusion(f32[6,64,768]{1,0,2:T(8,128)S(1)} %copy-done.3, f32[768,64,6]{1,0,2:T(8,128)S(1)} %bitcast.864), kind=kOutput, calls=%fused_computation.264 | convolution fusion | flops 226492416 | bytes 14942208 | tf_op jit(solution)/shard_map/transpose(jvp(bsc,scn->bcn))/dot_general | solution.py:36
  2398.6 42.7 %fusion.193 = f32[768,64,64]{2,1,0:T(8,128)} fusion(f32[6,768,64]{2,1,0:T(8,128)S(1)} %copy-done.33, f32[6,64,768]{1,0,2:T(8,128)S(1)} %copy-done.14), kind=kOutput, calls=%fused_computation.285 | convolution fusion | flops 226492416 | bytes 14942208 | tf_op jit(solution)/shard_map/transpose(jvp(bcn,tcn->btc))/dot_general | solution.py:44
  2441.4 113.8 %fusion.7 = (f32[768,64]{1,0:T(8,128)S(1)}, f32[768,64]{1,0:T(8,128)}, f32[768,64]{1,0:T(8,128)S(1)}, f32[768,64]{1,0:T(8,128)}, f32[768,64]{1,0:T(8,128)S(1)}, ...) fusion(f32[768,64]{1,0:T(8,128)} %get-tuple-element.1413, ...), kind=kOutput, calls=%fused_computation.49 | convolution fusion | flops 358023168 | bytes 44434176 | tf_op jit(solution)/shard_map/transpose(jvp(bcn,tcn->btc))/dot_general | solution.py:44
  2557.7 112.1 %fusion.15 = (f32[768,64]{1,0:T(8,128)S(1)}, f32[768,64]{1,0:T(8,128)S(1)}, f32[768,64]{1,0:T(8,128)S(1)}, f32[768,64]{1,0:T(8,128)S(1)}, f32[768,64]{1,0:T(8,12...) fusion(f32[768,64]{1,0:T(8,128)} %copy-done.154, ...), kind=kOutput, calls=%fused_computation.61 | convolution fusion | flops 358023168 | bytes 44434176 | tf_op jit(solution)/shard_map/transpose(jvp(bcn,tcn->btc))/dot_general | solution.py:44
  2687.1 80.5 %all-reduce.27 = (f32[3072]{0:T(1024)S(1)}, f32[3072]{0:T(1024)S(1)}, f32[1,2,768]{2,1,0:T(2,128)S(1)}, f32[1,2,768]{2,1,0:T(2,128)S(1)}, f32[1,2,768]{2,1,0:T(2...) all-reduce(f32[3072]{0:T(1024)S(1)} %fusion.196, ...), channel_id=1, replica_groups=mesh['dp'=4,'row'=4,'col'=2] {'dp','row'}, use_global_device_ids=true, to_apply=%region_49.52 | all-reduce | flops 15360 | bytes 122880 | tf_op jit(solution)/shard_map/psum | solution.py:235
  2774.0 37.5 %all-reduce.26 = (f32[1,768]{1,0:T(1,128)S(1)}, f32[1,768]{1,0:T(1,128)S(1)}, f32[1,768]{1,0:T(1,128)S(1)}, f32[1,768]{1,0:T(1,128)S(1)}, f32[1,768]{1,0:T(1,128)S(1)}, /*index=5*/f32[1,768]{1,0:T(1,128)S(1)}) all-reduce(f32[1,768]{1,0:T(1,128)S(1)} %stack.164, ...), channel_id=1, replica_groups=mesh['dp'=4,'row'=4,'col'=2] {'dp','row','col'}, use_global_device_ids=true, to_apply=%region_37.40 | all-reduce | flops 4608 | bytes 36864 | tf_op jit(solution)/shard_map/psum | solution.py:247
  2815.4 51.2 %all-reduce.33.cloned.1.call-done = (f32[1,2,768,64]{3,2,1,0:T(8,128)}, f32[1,2,768,64]{3,2,1,0:T(8,128)}, f32[1,2,768,64]{3,2,1,0:T(8,128)}, f32[1,2,768,64]{3,...) async-done(((f32[1,2,768,64]{3,2,1,0:T(8,128)}, f32[1,2,768,64]{3,2,1,0:T(8,128)}, f32[1,2,768,64]{3,2,1,0:T(8,128)}, f32[1,2,768,64]{3,2,1,0:T(8,128)}, ...) | async-done | bytes 2359312 | tf_op jit(solution)/shard_map/psum | solution.py:235
  2873.9 130.4 %all-reduce.35.cloned.1.call-done = (bf16[192,3072]{1,0:T(8,128)(2,1)}, bf16[192,3072]{1,0:T(8,128)(2,1)}, bf16[1,384,1536]{2,1,0:T(8,128)(2,1)}, bf16[1,384,153...) async-done(((bf16[192,3072]{1,0:T(8,128)(2,1)}, bf16[192,3072]{1,0:T(8,128)(2,1)}, bf16[1,384,1536]{2,1,0:T(8,128)(2,1)}, ...) | async-done | bytes 5898256 | tf_op jit(solution)/shard_map/psum | solution.py:231
  (965 shorter events, 718.0 us)
Async XLA Ops:
  7.2 141.5 %all-gather.29.cloned.1.call-start = ((), (), s32[]{:S(2)}) async-start(), calls=%async_computation.27 | async-start | bytes 1474560 | tf_op jit(solution)/shard_map/all_gather | solution.py:112
  9.6 139.1 %all-gather.27.cloned.1.call-start = ((), (), s32[]{:S(2)}) async-start(), calls=%async_computation.26 | async-start | bytes 1474560 | tf_op jit(solution)/shard_map/all_gather | solution.py:111
  10.6 138.1 %all-gather.31.cloned.1.call-start = ((), (), s32[]{:S(2)}) async-start(), calls=%async_computation.28 | async-start | bytes 2949120 | tf_op jit(solution)/shard_map/all_gather | solution.py:113
  12.0 479.0 %all-gather.23.cloned.1.call-start = ((), (), s32[]{:S(2)}) async-start(), calls=%async_computation.12 | async-start | bytes 1769472 | tf_op jit(solution)/shard_map/all_gather | solution.py:131
  166.0 62.7 %copy-start = (f32[6,64,768]{1,0,2:T(8,128)}, f32[6,64,768]{1,0,2:T(8,128)S(1)}, u32[]{:S(2)}) copy-start(f32[6,64,768]{1,0,2:T(8,128)S(1)} %copy.262) | copy-start | bytes 3538948
  327.1 44.4 %copy-start.2 = (f32[6,64,768]{1,0,2:T(8,128)}, f32[6,64,768]{1,0,2:T(8,128)S(1)}, u32[]{:S(2)}) copy-start(f32[6,64,768]{1,0,2:T(8,128)S(1)} %copy.252) | copy-start | bytes 3538948
  327.1 44.4 %copy-start.159 = (f32[768,64]{1,0:T(8,128)S(1)}, f32[768,64]{1,0:T(8,128)}, u32[]{:S(2)}) copy-start(f32[768,64]{1,0:T(8,128)} %copy-done.158) | copy-start | bytes 589828
  327.1 44.4 %copy-start.163 = (f32[768,64]{1,0:T(8,128)S(1)}, f32[768,64]{1,0:T(8,128)}, u32[]{:S(2)}) copy-start(f32[768,64]{1,0:T(8,128)} %get-tuple-element.1420) | copy-start | bytes 589828
  327.1 44.4 %copy-start.244 = (f32[64]{0:T(128)S(1)}, f32[64]{0:T(128)}, u32[]{:S(2)}) copy-start(f32[64]{0:T(128)} %get-tuple-element.1423) | copy-start | bytes 772
  426.8 46.2 %copy-start.32 = (f32[6,768,64]{2,1,0:T(8,128)}, f32[6,768,64]{2,1,0:T(8,128)S(1)}, u32[]{:S(2)}) copy-start(f32[6,768,64]{2,1,0:T(8,128)S(1)} %get-tuple-element.1922) | copy-start | bytes 3538948
  478.9 104.6 %all-gather.33.cloned.1.call-start = ((), (), s32[]{:S(2)}) async-start(), calls=%async_computation.29 | async-start | bytes 5898240 | tf_op jit(solution)/shard_map/all_gather | solution.py:133
  483.2 151.3 %all-gather.35.cloned.1.call-start = ((), (), s32[]{:S(2)}) async-start(), calls=%async_computation.30 | async-start | bytes 2949120 | tf_op jit(solution)/shard_map/all_gather | solution.py:134
  485.3 240.4 %reduce-scatter.13.cloned.1.call-start = ((), (), s32[]{:S(2)}) async-start(), calls=%async_computation.13 | async-start | bytes 884736 | tf_op jit(solution)/shard_map/reduce_scatter | solution.py:141
  638.1 94.8 %all-gather.39.cloned.1.call-start = ((), (), s32[]{:S(2)}) async-start(), calls=%async_computation.32 | async-start | bytes 1474560 | tf_op jit(solution)/shard_map/all_gather | solution.py:112
  638.9 94.0 %all-gather.37.cloned.1.call-start = ((), (), s32[]{:S(2)}) async-start(), calls=%async_computation.31 | async-start | bytes 1474560 | tf_op jit(solution)/shard_map/all_gather | solution.py:111
  639.6 122.3 %all-gather.41.cloned.1.call-start = ((), (), s32[]{:S(2)}) async-start(), calls=%async_computation.33 | async-start | bytes 2949120 | tf_op jit(solution)/shard_map/all_gather | solution.py:113
  640.2 461.1 %all-gather.45.cloned.1.call-start = ((), (), s32[]{:S(2)}) async-start(), calls=%async_computation.35 | async-start | bytes 2949120 | tf_op jit(solution)/shard_map/all_gather | solution.py:134
  640.9 464.7 %all-gather.43.cloned.1.call-start = ((), (), s32[]{:S(2)}) async-start(), calls=%async_computation.34 | async-start | bytes 5898240 | tf_op jit(solution)/shard_map/all_gather | solution.py:133
  641.5 465.5 %all-gather.25.cloned.1.call-start = ((), (), s32[]{:S(2)}) async-start(), calls=%async_computation.14 | async-start | bytes 1769472 | tf_op jit(solution)/shard_map/all_gather | solution.py:131
  641.7 87.2 %copy-start.193 = (f32[192]{0:T(256)}, f32[192]{0:T(256)S(1)}, u32[]{:S(2)}) copy-start(f32[192]{0:T(256)S(1)} %dynamic_slice.92) | copy-start | bytes 2308
  642.3 86.6 %copy-start.171 = (f32[768]{0:T(1024)}, f32[768]{0:T(1024)S(1)}, u32[]{:S(2)}) copy-start(f32[768]{0:T(1024)S(1)} %get-tuple-element.1157) | copy-start | bytes 9220
  778.3 44.5 %copy-start.4 = (f32[6,64,768]{1,0,2:T(8,128)}, f32[6,64,768]{1,0,2:T(8,128)S(1)}, u32[]{:S(2)}) copy-start(f32[6,64,768]{1,0,2:T(8,128)S(1)} %copy.282) | copy-start | bytes 3538948
  778.4 44.4 %copy-start.152 = (f32[768,64]{1,0:T(8,128)S(1)}, f32[768,64]{1,0:T(8,128)}, u32[]{:S(2)}) copy-start(f32[768,64]{1,0:T(8,128)} %get-tuple-element.1325) | copy-start | bytes 589828
  778.4 44.4 %copy-start.155 = (f32[768,64]{1,0:T(8,128)S(1)}, f32[768,64]{1,0:T(8,128)}, u32[]{:S(2)}) copy-start(f32[768,64]{1,0:T(8,128)} %copy-done.154) | copy-start | bytes 589828
  778.4 44.4 %copy-start.245 = (f32[64]{0:T(128)S(1)}, f32[64]{0:T(128)}, u32[]{:S(2)}) copy-start(f32[64]{0:T(128)} %get-tuple-element.1423) | copy-start | bytes 772
  968.8 44.8 %copy-start.23 = (f32[768,64]{1,0:T(8,128)S(1)}, f32[768,64]{1,0:T(8,128)}, u32[]{:S(2)}) copy-start(f32[768,64]{1,0:T(8,128)} %get-tuple-element.1864) | copy-start | bytes 589828
  1098.8 32.8 %reduce-scatter.17.cloned.1.call-start = ((), (), s32[]{:S(2)}) async-start(), calls=%async_computation.16 | async-start | bytes 1769472 | tf_op jit(solution)/shard_map/reduce_scatter | solution.py:193
  1121.7 313.4 %reduce-scatter.19.cloned.1.call-start = ((), (), s32[]{:S(2)}) async-start(), calls=%async_computation.17 | async-start | bytes 884736 | tf_op jit(solution)/shard_map/reduce_scatter | solution.py:208
  1370.5 44.5 %copy-start.43 = (f32[6,768,64]{2,1,0:T(8,128)}, f32[6,768,64]{2,1,0:T(8,128)S(1)}, u32[]{:S(2)}) copy-start(f32[6,768,64]{2,1,0:T(8,128)S(1)} %get-tuple-element.751) | copy-start | bytes 3538948
  1422.7 60.9 %copy-start.95 = (f32[384,768]{1,0:T(8,128)}, f32[384,768]{1,0:T(8,128)S(1)}, u32[]{:S(2)}) copy-start(f32[384,768]{1,0:T(8,128)S(1)} %get-tuple-element.1343) | copy-start | bytes 3538948
  1422.7 60.9 %copy-start.97 = (f32[384,768]{1,0:T(8,128)}, f32[384,768]{1,0:T(8,128)S(1)}, u32[]{:S(2)}) copy-start(f32[384,768]{1,0:T(8,128)S(1)} %get-tuple-element.1344) | copy-start | bytes 3538948
  1425.7 21.4 reduce-scatter.15.cloned.1.call-start
  1429.9 161.9 %reduce-scatter.21.cloned.1.call-start = ((), (), s32[]{:S(2)}) async-start(), calls=%async_computation.18 | async-start | bytes 1769472 | tf_op jit(solution)/shard_map/reduce_scatter | solution.py:193
  1468.1 1213.2 %reduce-scatter.35.cloned.1.call-start = ((), (), s32[]{:S(2)}) async-start(), calls=%async_computation.25 | async-start | bytes 2949120 | tf_op jit(solution)/shard_map/reduce_scatter | solution.py:226
  1472.5 1209.0 %reduce-scatter.33.cloned.1.call-start = ((), (), s32[]{:S(2)}) async-start(), calls=%async_computation.24 | async-start | bytes 2949120 | tf_op jit(solution)/shard_map/reduce_scatter | solution.py:226
  1476.7 1204.8 %reduce-scatter.31.cloned.1.call-start = ((), (), s32[]{:S(2)}) async-start(), calls=%async_computation.23 | async-start | bytes 5898240 | tf_op jit(solution)/shard_map/reduce_scatter | solution.py:223
  1483.5 1198.0 %reduce-scatter.27.cloned.1.call-start = ((), (), s32[]{:S(2)}) async-start(), calls=%async_computation.21 | async-start | bytes 5898240 | tf_op jit(solution)/shard_map/reduce_scatter | solution.py:220
  1491.1 1190.4 %reduce-scatter.29.cloned.1.call-start = ((), (), s32[]{:S(2)}) async-start(), calls=%async_computation.22 | async-start | bytes 5898240 | tf_op jit(solution)/shard_map/reduce_scatter | solution.py:223
  1492.9 64.8 %copy-start.215 = (s32[4096]{0:T(1024)}, s32[4096]{0:T(1024)S(1)}, u32[]{:S(2)}) copy-start(s32[4096]{0:T(1024)S(1)} %reshape.1325) | copy-start | bytes 49156
  1536.6 50.8 %copy-start.241 = (bf16[384,1536]{1,0:T(8,128)(2,1)S(1)}, bf16[384,1536]{1,0:T(8,128)(2,1)}, u32[]{:S(2)}) copy-start(bf16[384,1536]{1,0:T(8,128)(2,1)} %all-gather.23.cloned.1.call-done) | copy-start | bytes 3538948
  1536.6 50.8 %copy-start.258 = (bf16[384,1536]{1,0:T(8,128)(2,1)S(1)}, bf16[384,1536]{1,0:T(8,128)(2,1)}, u32[]{:S(2)}) copy-start(bf16[384,1536]{1,0:T(8,128)(2,1)} %copy-done.257) | copy-start | bytes 3538948
  1591.8 1089.8 %reduce-scatter.25.cloned.1.call-start = ((), (), s32[]{:S(2)}) async-start(), calls=%async_computation.20 | async-start | bytes 5898240 | tf_op jit(solution)/shard_map/reduce_scatter | solution.py:220
  1893.6 877.8 %reduce-scatter.23.cloned.1.call-start = ((), (), s32[]{:S(2)}) async-start(), calls=%async_computation.19 | async-start | bytes 884736 | tf_op jit(solution)/shard_map/reduce_scatter | solution.py:208
  1939.1 50.5 %copy-start.9 = (f32[6,64,768]{1,0,2:T(8,128)S(1)}, f32[6,64,768]{1,0,2:T(8,128)}, u32[]{:S(2)}) copy-start(f32[6,64,768]{1,0,2:T(8,128)} %copy-done.7) | copy-start | bytes 3538948
  2441.3 425.4 %all-reduce.33.cloned.1.call-start = ((), (), s32[]{:S(2)}) async-start(), calls=%async_computation.36 | async-start | bytes 9437184 | tf_op jit(solution)/shard_map/psum | solution.py:235
  2441.4 113.8 %copy-start.60 = (f32[1,1,768,64]{3,2,1,0:T(8,128)S(1)}, f32[1,1,768,64]{3,2,1,0:T(8,128)}, u32[]{:S(2)}) copy-start(f32[1,1,768,64]{3,2,1,0:T(8,128)} %copy-done.59) | copy-start | bytes 589828
  2441.4 113.8 %copy-start.86 = (f32[1,1,768,64]{3,2,1,0:T(8,128)S(1)}, f32[1,1,768,64]{3,2,1,0:T(8,128)}, u32[]{:S(2)}) copy-start(f32[1,1,768,64]{3,2,1,0:T(8,128)} %copy.363) | copy-start | bytes 589828
  2441.4 113.8 %copy-start.89 = (f32[1,1,768,64]{3,2,1,0:T(8,128)S(1)}, f32[1,1,768,64]{3,2,1,0:T(8,128)}, u32[]{:S(2)}) copy-start(f32[1,1,768,64]{3,2,1,0:T(8,128)} %copy.368) | copy-start | bytes 589828
  2441.4 113.8 %copy-start.185 = (f32[768]{0:T(1024)S(1)}, f32[768]{0:T(1024)}, u32[]{:S(2)}) copy-start(f32[768]{0:T(1024)} %copy-done.184) | copy-start | bytes 9220
  2555.2 114.6 %copy-start.112 = (f32[768,64]{1,0:T(8,128)}, f32[768,64]{1,0:T(8,128)S(1)}, u32[]{:S(2)}) copy-start(f32[768,64]{1,0:T(8,128)S(1)} %get-tuple-element.1135) | copy-start | bytes 589828
  2555.2 114.6 %copy-start.114 = (f32[768,64]{1,0:T(8,128)}, f32[768,64]{1,0:T(8,128)S(1)}, u32[]{:S(2)}) copy-start(f32[768,64]{1,0:T(8,128)S(1)} %get-tuple-element.1137) | copy-start | bytes 589828
  2557.7 112.1 %copy-start.58 = (f32[1,1,768,64]{3,2,1,0:T(8,128)S(1)}, f32[1,1,768,64]{3,2,1,0:T(8,128)}, u32[]{:S(2)}) copy-start(f32[1,1,768,64]{3,2,1,0:T(8,128)} %copy-done.57) | copy-start | bytes 589828
  2557.7 112.1 %copy-start.84 = (f32[1,1,768,64]{3,2,1,0:T(8,128)S(1)}, f32[1,1,768,64]{3,2,1,0:T(8,128)}, u32[]{:S(2)}) copy-start(f32[1,1,768,64]{3,2,1,0:T(8,128)} %copy-done.82) | copy-start | bytes 589828
  2557.7 112.1 %copy-start.85 = (f32[1,1,768,64]{3,2,1,0:T(8,128)S(1)}, f32[1,1,768,64]{3,2,1,0:T(8,128)}, u32[]{:S(2)}) copy-start(f32[1,1,768,64]{3,2,1,0:T(8,128)} %copy.367) | copy-start | bytes 589828
  2557.7 112.2 %copy-start.188 = (f32[768]{0:T(1024)S(1)}, f32[768]{0:T(1024)}, u32[]{:S(2)}) copy-start(f32[768]{0:T(1024)} %copy-done.187) | copy-start | bytes 9220
  2681.3 322.9 %all-reduce.35.cloned.1.call-start = ((), (), s32[]{:S(2)}) async-start(), calls=%async_computation.37 | async-start | bytes 11796480 | tf_op jit(solution)/shard_map/psum | solution.py:231
  2686.5 84.9 %copy-start.29 = (bf16[192,768]{1,0:T(8,128)(2,1)S(1)}, bf16[192,768]{1,0:T(8,128)(2,1)}, u32[]{:S(2)}) copy-start(bf16[192,768]{1,0:T(8,128)(2,1)} %param.40) | copy-start | bytes 884740
  2686.5 84.9 %copy-start.174 = (f32[768]{0:T(1024)S(1)}, f32[768]{0:T(1024)}, u32[]{:S(2)}) copy-start(f32[768]{0:T(1024)} %copy-done.173) | copy-start | bytes 9220
  2686.5 84.9 %copy-start.197 = (f32[192]{0:T(256)S(1)}, f32[192]{0:T(256)}, u32[]{:S(2)}) copy-start(f32[192]{0:T(256)} %copy-done.196) | copy-start | bytes 2308
  2686.5 86.1 %copy-start.227 = (f32[192]{0:T(256)S(1)}, f32[192]{0:T(256)}, u32[]{:S(2)}) copy-start(f32[192]{0:T(256)} %copy-done.226) | copy-start | bytes 2308
  2686.5 86.1 %copy-start.205 = (f32[192]{0:T(256)S(1)}, f32[192]{0:T(256)}, u32[]{:S(2)}) copy-start(f32[192]{0:T(256)} %copy-done.204) | copy-start | bytes 2308
  2686.8 126.5 %copy-start.92 = (f32[192,768]{1,0:T(8,128)S(1)}, f32[192,768]{1,0:T(8,128)}, u32[]{:S(2)}) copy-start(f32[192,768]{1,0:T(8,128)} %copy-done.91) | copy-start | bytes 1769476
  2686.9 126.5 %copy-start.104 = (bf16[192,768]{1,0:T(8,128)(2,1)S(1)}, bf16[192,768]{1,0:T(8,128)(2,1)}, u32[]{:S(2)}) copy-start(bf16[192,768]{1,0:T(8,128)(2,1)} %param.42) | copy-start | bytes 884740
  2686.9 126.5 %copy-start.225 = (f32[192]{0:T(256)S(1)}, f32[192]{0:T(256)}, u32[]{:S(2)}) copy-start(f32[192]{0:T(256)} %copy-done.224) | copy-start | bytes 2308
  (221 other events, 2798.9 us)
Sparse Core Ops, SparseCore 0:
  10.2 33.1 all-gather.28
  45.5 29.5 all-gather.26
  77.2 49.5 all-gather.30
  479.0 11.8 all-gather.22
  492.9 90.5 all-gather.32
  585.5 48.9 all-gather.34
  638.2 6.8 reduce-scatter.12
  647.3 31.5 all-gather.38
  680.6 29.5 all-gather.36
  712.3 49.5 all-gather.40
  764.1 49.2 all-gather.44
  815.0 88.2 all-gather.42
  1098.9 8.0 all-gather.24
  1121.8 9.8 reduce-scatter.16
  1425.9 9.2 reduce-scatter.18
  1437.9 9.1 reduce-scatter.14
  1468.3 9.8 reduce-scatter.20
  1480.4 49.1 reduce-scatter.34
  1532.1 47.5 reduce-scatter.32
  1581.9 84.7 reduce-scatter.30
  1669.1 85.7 reduce-scatter.26
  1757.3 85.7 reduce-scatter.28
  1893.7 86.3 reduce-scatter.24
  2441.4 9.1 reduce-scatter.22
  2681.4 185.2 all-reduce.32
  2871.6 132.6 all-reduce.34
where the time goes:
time: 3040 us; the launch traced here: 3020 us
  matrix products  1590 us (52%)
  local copies, waits for them, and re-layouts  520 us (17%)
  waiting for transfers between devices  382 us (13%)
  other arithmetic  379 us (12%)
  blocking collectives  127 us (4%)
    dot_general x12, matrix products, ssm_scan(): carried = jnp.einsum('bcn,tcn->btc', block_starts, head, precision=HIGH)  591 us
    dot_general x12, matrix products, ssm_scan(): block_ends = jnp.einsum('bsc,scn->bcn', blocks, tail, precision=HIGH)  457 us
    dot_general x12, matrix products, ssm_scan(): inside = jnp.einsum('tsc,bsc->btc', toeplitz, blocks, precision=HIGH)  452 us
    gather x8, local copies, waits for them, and re-layouts, ssm_scan(): jnp.take(kernel, lag_index, axis=0)  166 us
    psum x1, waiting for transfers between devices, body(): lax.psum(row_in.astype(jnp.bfloat16), 'dp').astype(jnp.float32)  130 us
    scatter-add x4, other arithmetic, ssm_scan(): jnp.take(kernel, lag_index, axis=0)  114 us
    dynamic_slice x48, local copies, waits for them, and re-layouts, ssm_scan(): lax.scan(advance, jnp.zeros_like(decay_rate), block_ends)  108 us
    all_gather x2, waiting for transfers between devices, body(): lax.all_gather(w_mix[depth_index].astype(jnp.bfloat16), 'row', axis=0, ti...  92.6 us
  transfers between devices with their start and end apart: 26, of which 10 were waited for; matrix products, arithmetic and copies ran while one was open for 60% of the time, Pallas kernels for 0%

commit v1 on v0

v1 whole, which is shorter than its diff:
```python
import functools

import jax
import jax.numpy as jnp
import numpy as np
from jax import lax
from jax.experimental import pallas as pl
from jax.experimental.pallas import tpu as pltpu
from jax.sharding import PartitionSpec as P

LAYERS = 2
EPS = 1e-05
LAG = 64
BF = jnp.bfloat16
F32 = jnp.float32
MESH = pl.DeviceIdType.MESH
VMEM_LIMIT = 60 * 1024 * 1024
CHUNK = 32


def transform_matrix(length):
    k = np.arange(length)[:, None]
    t = np.arange(length)[None, :]
    angle = np.pi * (((2 * k + 1) * t) % (4 * length)) / (2 * length)
    return np.concatenate((np.cos(angle), -np.sin(angle)), axis=0)


def gelu_only(v):
    t = jnp.tanh(v * (0.7978845608 + 0.035677408 * v * v))
    return (0.5 * v) * (1.0 + t)


def gelu_parts(v):
    sq = v * v
    t = jnp.tanh(v * (0.7978845608 + 0.035677408 * sq))
    half = 0.5 + 0.5 * t
    slope = half + (v * half) * (1.0 - t) * (0.7978845608 + 0.107032225 * sq)
    return v * half, slope


def dot(a, b, ca, cb):
    return lax.dot_general(a, b, (((ca,), (cb,)), ((), ())), preferred_element_type=F32)


def over_rows(rows, step, work):
    def one(i, unused):
        work(pl.ds(pl.multiple_of(i * step, step), step))
        return unused

    lax.fori_loop(0, rows // step, one, 0)


class Place:
    def __init__(self, n):
        self.n = n
        self.d = lax.axis_index("dp")
        self.c = lax.axis_index("col")

    def greet(self):
        barrier = pltpu.get_barrier_semaphore()
        for k in range(1, self.n):
            pl.semaphore_signal(barrier, inc=1, device_id={"dp": self.ahead(k)}, device_id_type=MESH)
        pl.semaphore_signal(barrier, inc=1, device_id={"col": 1 - self.c}, device_id_type=MESH)
        pl.semaphore_wait(barrier, self.n)

    def ahead(self, k):
        return lax.rem(self.d + k, self.n)

    def behind(self, k):
        return lax.rem(self.d - k + self.n, self.n)

    def other(self, i):
        return i + (i + self.n - self.d) // self.n

    def to_dp(self, src, dst, send, recv, q):
        return pltpu.make_async_remote_copy(
            src, dst, send, recv, device_id={"dp": q}, device_id_type=MESH
        )

    def to_mate(self, src, dst, send, recv):
        return pltpu.make_async_remote_copy(
            src, dst, send, recv, device_id={"col": 1 - self.c}, device_id_type=MESH
        )


def gather_tokens(place, buf, rows, length, send_p, recv_p, send_m, recv_m):
    def region(slot):
        return buf.at[pl.ds(pl.multiple_of(slot * length + place.c * rows, rows), rows)]

    own = region(place.d)

    def peer(k):
        return place.to_dp(own, own, send_p.at[k], recv_p.at[k], place.ahead(k))

    def mate(k):
        part = region(place.behind(k))
        return place.to_mate(part, part, send_m.at[k], recv_m.at[k])

    def start():
        mate(0).start()
        for k in range(1, place.n):
            peer(k).start()

    def fetch(k):
        peer(k).wait_recv()
        forward = mate(k)
        forward.start()
        forward.wait_recv()

    def finish():
        def one(k, unused):
            peer(k).wait_send()
            mate(k).wait_send()
            return unused

        mate(0).wait_send()
        lax.fori_loop(1, place.n, one, 0)

    return start, lambda: mate(0).wait_recv(), fetch, finish


def norm_stats(residual):
    mean = jnp.mean(residual, axis=1, keepdims=True)
    centered = residual - mean
    variance = jnp.mean(centered * centered, axis=1, keepdims=True)
    inv = lax.rsqrt(variance + EPS)
    return centered * inv, inv


def sum_to_owner(place, rows, mate_out, mate_in, sum_out, sum_in, own, send_m, recv_m, send_p, recv_p):
    def to_mate(slot):
        return place.to_mate(mate_out.at[slot], mate_in.at[slot], send_m.at[slot], recv_m.at[slot])

    def to_owner(slot):
        k = lax.rem(slot - place.d + place.n, place.n)
        return place.to_dp(sum_out.at[slot], sum_in.at[k], send_p.at[k], recv_p.at[k], slot)

    def close(slot, mine):
        to_mate(slot).wait_recv()

        def work(r):
            own[mine, r] = own[mine, r] + mate_in[slot, r].astype(F32)

        over_rows(rows, 16, work)

        @pl.when(slot != place.d)
        def _():
            sum_out[slot] = own[mine].astype(BF)
            to_owner(slot).start()

    def receive():
        def one(k, unused):
            to_owner(place.ahead(k)).wait_recv()
            return unused

        lax.fori_loop(1, place.n, one, 0)

    def finish():
        def one(k, unused):
            to_owner(place.ahead(k)).wait_send()
            return unused

        lax.fori_loop(1, place.n, one, 0)

        def two(s, unused):
            to_mate(s).wait_send()
            return unused

        lax.fori_loop(0, place.n, two, 0)

    return to_mate, close, receive, finish


def fwd_kernel(
    n, res_ref, gain_ref, shift_ref, mask_ref, own_mask_ref, w_in_ref, w_mx_ref, w_out_ref, in_bias_ref,
    mix_bias_ref, out_bias_ref, kre_ref, kim_ref, ft_ref, f_ref,
    new_ref, g_out, mx_out, pre_out, u_out, y_out, pm_out, prod_out,
    w_in_t, w_mx_t, g, mx, pre, u_sp, y, pm, prod, act, spec, y_hat, prod_f, prod_t,
    own, mate_out, mate_in, sum_out, sum_in,
    send_a, recv_a, send_am, recv_am, send_b, recv_b, send_bm, recv_bm, send_c, recv_c, send_cm, recv_cm, save,
):
    place = Place(n)
    d, c = place.d, place.c
    rows, width = res_ref.shape
    length = mask_ref.shape[2]
    hid = w_mx_ref.shape[1]
    ch2 = kre_ref.shape[0]
    ch = ch2 // 2

    place.greet()
    start_a, own_a, fetch_a, finish_a = gather_tokens(place, g, rows, length, send_a, recv_a, send_am, recv_am)
    base = d * length + c * rows

    def norm(r):
        xhat, _ = norm_stats(res_ref[r])
        at = pl.ds(pl.multiple_of(base + r.start, 16), 16)
        g[at] = (xhat * gain_ref[...] + shift_ref[...]).astype(BF)

    over_rows(rows, 16, norm)
    start_a()

    def turn_in(r):
        w_in_t[r] = w_in_ref[:, r].astype(F32).T.astype(BF)

    over_rows(w_in_ref.shape[1], 128, turn_in)

    def turn_mx(r):
        w_mx_t[:, r] = w_mx_ref[r].astype(F32).T.astype(BF)

    over_rows(w_mx_ref.shape[0], 128, turn_mx)
    own_a()

    def chunk(owner, slot):
        at = pl.ds(pl.multiple_of((c * n + owner) * ch, ch), ch)
        return mx.at[at, pl.ds(pl.multiple_of(slot * length, length), length)]

    def peer_b(k, slot):
        part = chunk(d, slot)
        return place.to_dp(part, part, send_b.at[slot, k], recv_b.at[slot, k], place.ahead(k))

    def mate_b(k, slot):
        part = chunk(place.behind(k), slot)
        return place.to_mate(part, part, send_bm.at[slot, k], recv_bm.at[slot, k])

    def saves(slot, item):
        lanes = pl.ds(pl.multiple_of(slot * length, length), length)
        src, dst = (
            lambda: (g.at[lanes], g_out.at[lanes]),
            lambda: (u_sp.at[slot], u_out.at[slot]),
            lambda: (y.at[slot], y_out.at[slot]),
            lambda: (pre.at[slot], pre_out.at[slot]),
            lambda: (mx.at[:, lanes], mx_out.at[:, lanes]),
            lambda: (pm.at[slot], pm_out.at[slot]),
            lambda: (prod.at[:, lanes], prod_out.at[:, lanes]),
        )[item]()
        return pltpu.make_async_copy(src, dst, save.at[item, slot])

    def scan_slot(i, unused):
        slot = lax.select(i == 0, d, place.other(i - 1))

        @pl.when(i > 0)
        def _():
            fetch_a(lax.rem(d - slot + n, n))

        lanes = pl.ds(pl.multiple_of(slot * length, length), length)
        pre[slot] = dot(w_in_t[...], g[lanes], 1, 1)
        live = mask_ref[slot]

        def acts(r):
            v = pre[slot, r] + in_bias_ref[r]
            pre[slot, r] = v
            act[r] = (gelu_only(v) * live).astype(BF)

        over_rows(ch2, CHUNK, acts)

        def shift_value(r):
            at = pl.ds(pl.multiple_of(ch2 + r.start, CHUNK), CHUNK)
            pre[slot, at] = pre[slot, at] + in_bias_ref[at]

        over_rows(hid, CHUNK, shift_value)
        spec[...] = dot(act[...], ft_ref[...], 1, 0)

        def multiply(r):
            u_re, u_im = spec[r, :length], spec[r, length:]
            k_re, k_im = kre_ref[r], kim_ref[r]
            u_sp[slot, r, :length] = u_re.astype(BF)
            u_sp[slot, r, length:] = u_im.astype(BF)
            y_hat[r, :length] = (k_re * u_re - k_im * u_im).astype(BF)
            y_hat[r, length:] = (k_re * u_im + k_im * u_re).astype(BF)

        over_rows(ch2, 16, multiply)
        y[slot] = dot(y_hat[...], f_ref[...], 1, 0)
        mine = (c * n + d) * ch

        def mix(r):
            back = pl.ds(pl.multiple_of(ch + r.start, 16), 16)
            at = pl.ds(pl.multiple_of(mine + r.start, 16), 16)
            mx[at, lanes] = (y[slot, r] * y[slot, back]).astype(BF)

        over_rows(ch, 16, mix)
        mate_b(0, slot).start()
        for k in range(1, n):
            peer_b(k, slot).start()
        for item in range(4):
            saves(slot, item).start()
        return unused

    lax.fori_loop(0, n, scan_slot, 0)

    to_mate, close, receive, finish_c = sum_to_owner(
        place, rows, mate_out, mate_in, sum_out, sum_in, own, send_cm, recv_cm, send_c, recv_c
    )

    def order(i):
        return lax.select(i == n - 1, d, place.other(i))

    def hidden_slot(i, unused):
        slot = order(i)
        lanes = pl.ds(pl.multiple_of(slot * length, length), length)
        for k in range(1, n):
            peer_b(k, slot).wait_recv()
            mate_b(k, slot).start()
        for k in range(n):
            mate_b(k, slot).wait_recv()
        pm[slot] = dot(w_mx_t[...], mx[:, lanes], 1, 0)

        def gate(r):
            v = pm[slot, r] + mix_bias_ref[r]
            pm[slot, r] = v
            at = pl.ds(pl.multiple_of(ch2 + r.start, CHUNK), CHUNK)
            product = gelu_only(v) * gelu_only(pre[slot, at])
            prod_f[r] = product
            prod[r, lanes] = product.astype(BF)

        over_rows(hid, CHUNK, gate)
        prod_t[...] = prod_f[...].T.astype(BF)
        for item in range(4, 7):
            saves(slot, item).start()
        theirs = pl.ds(pl.multiple_of((1 - c) * rows, rows), rows)
        ours = pl.ds(pl.multiple_of(c * rows, rows), rows)
        mate_out[slot] = dot(prod_t[theirs], w_out_ref[...], 1, 0).astype(BF)
        to_mate(slot).start()

        @pl.when(i > 0)
        def _():
            close(order(i - 1), lax.rem(i - 1, 2))

        own[lax.rem(i, 2)] = dot(prod_t[ours], w_out_ref[...], 1, 0)
        return unused

    lax.fori_loop(0, n, hidden_slot, 0)
    last = (n - 1) % 2
    close(d, last)
    receive()

    def final(r):
        total = own[last, r]
        for k in range(1, n):
            total = total + sum_in[k, r].astype(F32)
        new_ref[r] = res_ref[r] + own_mask_ref[r] * (total + out_bias_ref[...])

    over_rows(rows, 16, final)
    finish_a()
    finish_c()

    def drain(slot, unused):
        for k in range(1, n):
            peer_b(k, slot).wait_send()
        for k in range(n):
            mate_b(k, slot).wait_send()
        for item in range(7):
            saves(slot, item).wait()
        return unused

    lax.fori_loop(0, n, drain, 0)


def bwd_kernel(
    n, grad_ref, res_ref, gain_ref, mask_ref, own_mask_ref, w_in_ref, w_mx_ref, w_out_ref, kre_ref, kim_ref,
    ft_ref, f_ref, g_in, mx_in, pre_in, u_in, y_in, pm_in, prod_in,
    new_ref, gw_in_ref, gw_mx_ref, gw_out_ref, in_sum_ref, mix_sum_ref, norm_sum_ref, dk_ref,
    gb, g, mx, pre, u_sp, y, pm, prod, gpre, gpre_f, gpm, gact, spec, hat, turned,
    mix_out, mix_mate, mix_own, mix_sum, mix_got,
    own, mate_out, mate_in, sum_out, sum_in,
    send_a, recv_a, send_am, recv_am, send_b, recv_b, send_bm, recv_bm, send_c, recv_c, send_cm, recv_cm, load,
):
    place = Place(n)
    d, c = place.d, place.c
    rows, width = res_ref.shape
    length = mask_ref.shape[2]
    hid = w_mx_ref.shape[1]
    ch2 = kre_ref.shape[0]
    ch = ch2 // 2
    half = n * ch

    def loads(slot, item):
        lanes = pl.ds(pl.multiple_of(slot * length, length), length)
        src, dst = (
            lambda: (pre_in.at[slot], pre.at[slot]),
            lambda: (pm_in.at[slot], pm.at[slot]),
            lambda: (y_in.at[slot], y.at[slot]),
            lambda: (u_in.at[slot], u_sp.at[slot]),
            lambda: (prod_in.at[:, lanes], prod.at[:, lanes]),
            lambda: (mx_in.at[:, lanes], mx.at[:, lanes]),
            lambda: (g_in.at[lanes], g.at[lanes]),
        )[item]()
        return pltpu.make_async_copy(src, dst, load.at[item, slot])

    for item in range(7):
        loads(d, item).start()

    def start_loads(i, unused):
        for item in range(7):
            loads(place.other(i), item).start()
        return unused

    lax.fori_loop(0, n - 1, start_loads, 0)

    place.greet()
    start_a, own_a, fetch_a, finish_a = gather_tokens(place, gb, rows, length, send_a, recv_a, send_am, recv_am)
    base = d * length + c * rows

    norm_sum_ref[...] = jnp.zeros_like(norm_sum_ref)

    def first(r):
        part = grad_ref[r] * own_mask_ref[r]
        at = pl.ds(pl.multiple_of(base + r.start, 16), 16)
        gb[at] = part.astype(BF)
        norm_sum_ref[2:3] = norm_sum_ref[2:3] + jnp.sum(part, axis=0, keepdims=True)

    over_rows(rows, 16, first)
    start_a()
    in_sum_ref[...] = jnp.zeros_like(in_sum_ref)
    mix_sum_ref[...] = jnp.zeros_like(mix_sum_ref)
    dk_ref[...] = jnp.zeros_like(dk_ref)
    own_a()

    def mate_b(slot):
        return place.to_mate(mix_out.at[slot], mix_mate.at[slot], send_bm.at[slot], recv_bm.at[slot])

    def peer_b(k, slot):
        q = place.ahead(k)
        part = mix_sum.at[slot, pl.ds(pl.multiple_of(q * ch, ch), ch)]
        return place.to_dp(part, mix_got.at[k, slot], send_b.at[slot, k], recv_b.at[slot, k], q)

    def hidden_slot(i, unused):
        slot = lax.select(i == 0, d, place.other(i - 1))

        @pl.when(i > 0)
        def _():
            fetch_a(lax.rem(d - slot + n, n))

        lanes = pl.ds(pl.multiple_of(slot * length, length), length)
        gact[...] = dot(w_out_ref[...], gb[lanes], 1, 1)
        for item in range(2):
            loads(slot, item).wait()

        def gates(r):
            at = pl.ds(pl.multiple_of(ch2 + r.start, 16), 16)
            gated, slope = gelu_parts(pm[slot, r])
            value, value_slope = gelu_parts(pre[slot, at])
            now = gact[r]
            to_value = now * gated * value_slope
            to_mix = now * value * slope
            gpre[at, lanes] = to_value.astype(BF)
            gpm[r, lanes] = to_mix.astype(BF)
            in_sum_ref[at] = in_sum_ref[at] + jnp.sum(to_value, axis=1, keepdims=True)
            mix_sum_ref[r] = mix_sum_ref[r] + jnp.sum(to_mix, axis=1, keepdims=True)

        over_rows(hid, 16, gates)
        theirs = pl.ds(pl.multiple_of((1 - c) * half, half), half)
        ours = pl.ds(pl.multiple_of(c * half, half), half)
        mix_out[slot] = dot(w_mx_ref[theirs], gpm[:, lanes], 1, 0).astype(BF)
        mate_b(slot).start()
        mix_own[...] = dot(w_mx_ref[ours], gpm[:, lanes], 1, 0)
        mate_b(slot).wait_recv()

        def add(r):
            mix_sum[slot, r] = (mix_own[r] + mix_mate[slot, r].astype(F32)).astype(BF)

        over_rows(half, 16, add)
        for k in range(1, n):
            peer_b(k, slot).start()
        return unused

    lax.fori_loop(0, n, hidden_slot, 0)

    def wait_loads(slot, unused):
        for item in range(2, 7):
            loads(slot, item).wait()
        return unused

    lax.fori_loop(0, n, wait_loads, 0)
    gw_out_ref[...] = dot(prod[...], gb[...], 1, 0).astype(BF)

    def grad_mix(r):
        gw_mx_ref[r] = dot(mx[r], gpm[...], 1, 1).astype(BF)

    over_rows(mx.shape[0], 256, grad_mix)

    to_mate, close, receive, finish_c = sum_to_owner(
        place, rows, mate_out, mate_in, sum_out, sum_in, own, send_cm, recv_cm, send_c, recv_c
    )

    def order(i):
        return lax.select(i == n - 1, d, place.other(i))

    def scan_slot(i, unused):
        slot = order(i)
        lanes = pl.ds(pl.multiple_of(slot * length, length), length)
        for k in range(1, n):
            peer_b(k, slot).wait_recv()

        def outer(r):
            at = pl.ds(pl.multiple_of(d * ch + r.start, 16), 16)
            back = pl.ds(pl.multiple_of(ch + r.start, 16), 16)
            total = mix_sum[slot, at].astype(F32)
            for k in range(1, n):
                total = total + mix_got[k, slot, r].astype(F32)
            hat[r, :length] = (total * y[slot, back]).astype(BF)
            hat[back, :length] = (total * y[slot, r]).astype(BF)

        over_rows(ch, 16, outer)
        spec[...] = dot(hat[:, :length], ft_ref[...], 1, 0)

        def multiply(r):
            g_re, g_im = spec[r, :length], spec[r, length:]
            k_re, k_im = kre_ref[r], kim_ref[r]
            hat[r, :length] = (k_re * g_re + k_im * g_im).astype(BF)
            hat[r, length:] = (k_re * g_im - k_im * g_re).astype(BF)
            u_re, u_im = u_sp[slot, r, :length].astype(F32), u_sp[slot, r, length:].astype(F32)
            dk_ref[r, :length] = dk_ref[r, :length] + (u_re * g_re + u_im * g_im)
            dk_ref[r, length:] = dk_ref[r, length:] + (u_re * g_im - u_im * g_re)

        over_rows(ch2, 16, multiply)
        spec[:, :length] = dot(hat[...], f_ref[...], 1, 0)
        live = mask_ref[slot]

        def inner(r):
            _, slope = gelu_parts(pre[slot, r])
            part = spec[r, :length] * slope * live
            gpre_f[r] = part
            gpre[r, lanes] = part.astype(BF)
            in_sum_ref[r] = in_sum_ref[r] + jnp.sum(part, axis=1, keepdims=True)

        over_rows(ch2, 16, inner)
        turned[:, :ch2] = gpre_f[...].T.astype(BF)
        gpre_f[...] = gpre[ch2:, lanes].astype(F32)
        turned[:, ch2:] = gpre_f[...].T.astype(BF)
        theirs = pl.ds(pl.multiple_of((1 - c) * rows, rows), rows)
        ours = pl.ds(pl.multiple_of(c * rows, rows), rows)
        mate_out[slot] = dot(turned[theirs], w_in_ref[...], 1, 1).astype(BF)
        to_mate(slot).start()

        @pl.when(i > 0)
        def _():
            close(order(i - 1), lax.rem(i - 1, 2))

        own[lax.rem(i, 2)] = dot(turned[ours], w_in_ref[...], 1, 1)
        return unused

    lax.fori_loop(0, n, scan_slot, 0)
    last = (n - 1) % 2
    close(d, last)

    def grad_in(r):
        gw_in_ref[:, r] = dot(gpre[r], g[...], 1, 0).T.astype(BF)

    over_rows(gpre.shape[0], 128, grad_in)
    receive()

    def final(r):
        total = own[last, r]
        for k in range(1, n):
            total = total + sum_in[k, r].astype(F32)
        xhat, inv = norm_stats(res_ref[r])
        h = total * gain_ref[...]
        middle = jnp.mean(h, axis=1, keepdims=True)
        along = jnp.mean(h * xhat, axis=1, keepdims=True)
        new_ref[r] = grad_ref[r] + inv * (h - middle - xhat * along)
        norm_sum_ref[0:1] = norm_sum_ref[0:1] + jnp.sum(total * xhat, axis=0, keepdims=True)
        norm_sum_ref[1:2] = norm_sum_ref[1:2] + jnp.sum(total, axis=0, keepdims=True)

    over_rows(rows, 16, final)
    finish_a()
    finish_c()

    def drain(slot, unused):
        mate_b(slot).wait_send()
        for k in range(1, n):
            peer_b(k, slot).wait_send()
        return unused

    lax.fori_loop(0, n, drain, 0)


def tables_kernel(decay_ref, step_ref, b_ref, c_ref, skip_ref, sign_ref, ft_ref, kre_ref, kim_ref, rate, lead):
    length = ft_ref.shape[0]
    blocks = length // LAG
    decay = decay_ref[0]
    rate[...] = jnp.exp(step_ref[0]) * jnp.exp(decay)
    weight = (1.0 - jnp.exp(-rate[...])) * jnp.exp(-decay) * b_ref[0] * c_ref[0]
    for b in range(blocks):
        lead[b] = weight * jnp.exp(-(LAG * b) * rate[...])
    lanes = rate.shape[1]
    offs = lax.broadcasted_iota(jnp.int32, (LAG, lanes), 0).astype(F32)

    def state(i, totals):
        powers = jnp.exp(-offs * rate[pl.ds(i, 1)])
        return tuple(totals[b] + powers * lead[b, pl.ds(i, 1)] for b in range(blocks))

    zero = jnp.zeros((LAG, lanes), F32)
    totals = list(lax.fori_loop(0, rate.shape[0], state, (zero,) * blocks))
    at_zero = lax.broadcasted_iota(jnp.int32, (LAG, lanes), 0) == 0
    totals[0] = totals[0] + jnp.where(at_zero, skip_ref[0], 0.0)
    kernel = jnp.concatenate(totals, axis=0)
    k_hat = dot(kernel.T.astype(BF), ft_ref[...], 1, 0) * (1.0 / length)
    kre_ref[0] = k_hat[:, :length]
    kim_ref[0] = k_hat[:, length:] * sign_ref[...]


def params_kernel(
    dk_ref, decay_ref, step_ref, b_ref, c_ref, sign_ref, ft_ref, g_decay, g_b, g_c, g_row, lag_sums
):
    length = ft_ref.shape[0]
    re = dk_ref[:, :length].astype(BF)
    im = (dk_ref[:, length:] * sign_ref[...]).astype(BF)
    lag_sums[...] = (dot(ft_ref[:, :length], re, 1, 1) + dot(ft_ref[:, length:], im, 1, 1)) * (1.0 / length)
    decay = decay_ref[...]
    rate = jnp.exp(step_ref[...]) * jnp.exp(decay)
    a = jnp.exp(-rate)

    def lag(i, carry):
        total, slope = carry
        row = lag_sums[pl.ds(length - 1 - i, 1)]
        return total * a + row, slope * a + total

    zero = jnp.zeros_like(a)
    total, slope = lax.fori_loop(0, length, lag, (zero, zero))
    inv_decay = jnp.exp(-decay)
    gain = (1.0 - a) * inv_decay
    b_in, c_out = b_ref[...], c_ref[...]
    b_disc = gain * b_in
    to_b = c_out * total
    to_rate = a * (to_b * inv_decay * b_in - (c_out * b_disc) * slope)
    through = to_rate * rate
    g_decay[...] = through - to_b * b_disc
    g_b[...] = to_b * gain
    g_c[...] = b_disc * total
    g_row[...] = jnp.zeros_like(g_row)
    g_row[0:1] = jnp.sum(through, axis=0, keepdims=True)
    g_row[1:2] = lag_sums[0:1]


VM = pl.BlockSpec(memory_space=pltpu.VMEM)
ANY = pl.BlockSpec(memory_space=pl.ANY)


def shape(dims, dtype):
    return jax.ShapeDtypeStruct(tuple(dims), dtype)


def sem(*dims):
    return pltpu.SemaphoreType.DMA(dims)


def body(
    tokens_in, lengths, cotangent, norm_gain, norm_shift, w_fwd, w_bwd, w_value, bias_fwd, bias_bwd,
    bias_value, decay_log, step_log, b_input, c_output, skip_gain, w_mix, bias_mix, w_output, bias_output,
):
    n = lax.axis_size("dp")
    cols = lax.axis_size("col")
    d = lax.axis_index("dp")
    rows, width = tokens_in.shape
    length = rows * cols
    ch = w_fwd.shape[2] // n
    ch2 = 2 * ch
    hid = w_mix.shape[2] // n
    wide = ch2 + hid
    chans = n * cols * ch
    tokens = n * length
    matrix = transform_matrix(length)
    f_mat = jnp.asarray(matrix, BF)
    ft_mat = jnp.asarray(np.ascontiguousarray(matrix.T), BF)

    def mine(x, size, axis):
        return lax.dynamic_slice_in_dim(x, d * size, size, axis)

    weights = []
    for l in range(LAYERS):
        w_in = jnp.concatenate(
            (mine(w_fwd[l], ch, 1), mine(w_bwd[l], ch, 1), mine(w_value[l], hid, 1)), axis=1
        ).astype(BF)
        w_in = lax.all_gather(w_in, "row", axis=0, tiled=True)
        w_mx = lax.all_gather(mine(w_mix[l], hid, 1).astype(BF), "row", axis=0, tiled=True)
        w_out = lax.all_gather(mine(w_output[l], hid, 0).astype(BF), "row", axis=1, tiled=True)
        in_bias = jnp.concatenate(
            (mine(bias_fwd[l], ch, 0), mine(bias_bwd[l], ch, 0), mine(bias_value[l], hid, 0))
        )[:, None]
        mix_bias = mine(bias_mix[l], hid, 0)[:, None]
        weights.append((w_in, w_mx, w_out, in_bias, mix_bias))

    all_lengths = lax.all_gather(lengths, "dp", axis=0, tiled=True)
    positions = jnp.arange(length, dtype=jnp.int32)
    mask = (positions[None, :] < all_lengths[:, None]).astype(F32)[:, None, :]
    own_mask = lax.dynamic_slice_in_dim(
        (positions < lengths[0]).astype(F32), lax.axis_index("col") * rows, rows, 0
    )[:, None]

    def states_first(x):
        part = mine(x, ch, 2)
        return part.transpose(0, 3, 1, 2).reshape(LAYERS, x.shape[3], ch2)

    def one_row(x):
        return mine(x, ch, 2).reshape(LAYERS, 1, ch2)

    decay_t, b_t, c_t = states_first(decay_log), states_first(b_input), states_first(c_output)
    step_t, skip_t = one_row(step_log), one_row(skip_gain)
    states = decay_t.shape[1]
    sign = jnp.where(jnp.arange(ch2) < ch, 1.0, -1.0).astype(F32)[:, None]
    lane = 128
    by_state = pl.BlockSpec((1, states, lane), lambda l, j: (l, 0, j))
    by_row = pl.BlockSpec((1, 1, lane), lambda l, j: (l, 0, j))
    by_sign = pl.BlockSpec((lane, 1), lambda l, j: (j, 0))
    by_chan = pl.BlockSpec((1, lane, length), lambda l, j: (l, j, 0))
    k_re, k_im = pl.pallas_call(
        tables_kernel,
        grid=(LAYERS, ch2 // lane),
        out_shape=(shape((LAYERS, ch2, length), F32),) * 2,
        in_specs=[by_state, by_row, by_state, by_state, by_row, by_sign,
                  pl.BlockSpec((length, 2 * length), lambda l, j: (0, 0))],
        out_specs=(by_chan, by_chan),
        scratch_shapes=[pltpu.VMEM((states, lane), F32), pltpu.VMEM((length // LAG, states, lane), F32)],
        name="tables",
    )(decay_t, step_t, b_t, c_t, skip_t, sign, ft_mat)

    comm = [
        sem(n), sem(n), sem(n), sem(n), sem(n, n), sem(n, n),
    ]
    sums = [
        pltpu.VMEM((2, rows, width), F32), pltpu.VMEM((n, rows, width), BF), pltpu.VMEM((n, rows, width), BF),
        pltpu.VMEM((n, rows, width), BF), pltpu.VMEM((n, rows, width), BF),
    ]
    saved_shapes = (
        shape((tokens, width), BF), shape((chans, tokens), BF), shape((n, wide, length), F32),
        shape((n, ch2, 2 * length), BF), shape((n, ch2, length), F32), shape((n, hid, length), F32),
        shape((hid, tokens), BF),
    )
    fwd = pl.pallas_call(
        functools.partial(fwd_kernel, n),
        out_shape=(shape((rows, width), F32), *saved_shapes),
        in_specs=[VM] * 15,
        out_specs=(VM, *([ANY] * 7)),
        scratch_shapes=[
            pltpu.VMEM((wide, width), BF), pltpu.VMEM((hid, chans), BF),
            *(pltpu.VMEM(s.shape, s.dtype) for s in saved_shapes),
            pltpu.VMEM((ch2, length), BF), pltpu.VMEM((ch2, 2 * length), F32), pltpu.VMEM((ch2, 2 * length), BF),
            pltpu.VMEM((hid, length), F32), pltpu.VMEM((length, hid), BF),
            *sums, *comm, sem(n, n), sem(n, n), sem(n), sem(n), sem(n), sem(n), sem(7, n),
        ],
        compiler_params=pltpu.CompilerParams(
            collective_id=0, has_side_effects=True, vmem_limit_bytes=VMEM_LIMIT
        ),
        name="forward_block",
    )
    bwd = pl.pallas_call(
        functools.partial(bwd_kernel, n),
        out_shape=(
            shape((rows, width), F32), shape((width, wide), BF), shape((chans, hid), BF), shape((hid, width), BF),
            shape((wide, 1), F32), shape((hid, 1), F32), shape((8, width), F32), shape((ch2, 2 * length), F32),
        ),
        in_specs=[VM] * 12 + [ANY] * 7,
        out_specs=(VM,) * 8,
        scratch_shapes=[
            pltpu.VMEM((tokens, width), BF),
            *(pltpu.VMEM(s.shape, s.dtype) for s in saved_shapes),
            pltpu.VMEM((wide, tokens), BF), pltpu.VMEM((ch2, length), F32), pltpu.VMEM((hid, tokens), BF),
            pltpu.VMEM((hid, length), F32), pltpu.VMEM((ch2, 2 * length), F32), pltpu.VMEM((ch2, 2 * length), BF),
            pltpu.VMEM((length, wide), BF),
            pltpu.VMEM((n, n * ch, length), BF), pltpu.VMEM((n, n * ch, length), BF),
            pltpu.VMEM((n * ch, length), F32), pltpu.VMEM((n, n * ch, length), BF),
            pltpu.VMEM((n, n, ch, length), BF),
            *sums, *comm, sem(n), sem(n), sem(n), sem(n), sem(n), sem(n), sem(7, n),
        ],
        compiler_params=pltpu.CompilerParams(
            collective_id=1, has_side_effects=True, vmem_limit_bytes=VMEM_LIMIT
        ),
        name="backward_block",
    )

    residual = tokens_in.astype(F32)
    stored = []
    for l in range(LAYERS):
        w_in, w_mx, w_out, in_bias, mix_bias = weights[l]
        new, *saved = fwd(
            residual, norm_gain[l][None], norm_shift[l][None], mask, own_mask, w_in, w_mx, w_out, in_bias,
            mix_bias, bias_output[l][None], k_re[l], k_im[l], ft_mat, f_mat,
        )
        stored.append((residual, saved))
        residual = new
    tokens_out = residual.astype(BF)

    by_all = pl.BlockSpec((states, lane), lambda j: (0, j))
    params = pl.pallas_call(
        params_kernel,
        grid=(ch2 // lane,),
        out_shape=(shape((states, ch2), F32),) * 3 + (shape((8, ch2), F32),),
        in_specs=[
            pl.BlockSpec((lane, 2 * length), lambda j: (j, 0)), by_all, pl.BlockSpec((1, lane), lambda j: (0, j)),
            by_all, by_all, pl.BlockSpec((lane, 1), lambda j: (j, 0)),
            pl.BlockSpec((length, 2 * length), lambda j: (0, 0)),
        ],
        out_specs=(by_all, by_all, by_all, pl.BlockSpec((8, lane), lambda j: (0, j))),
        scratch_shapes=[pltpu.VMEM((length, lane), F32)],
        name="state_gradients",
    )

    def spread(x, axis):
        return lax.all_gather(x, "dp", axis=axis, tiled=True).astype(F32)

    grad = cotangent.astype(F32)
    outs = []
    for l in reversed(range(LAYERS)):
        w_in, w_mx, w_out, _, _ = weights[l]
        resid_in, saved = stored[l]
        grad, gw_in, gw_mix, gw_out, in_sum, mix_sum, norm_part, dk = bwd(
            grad, resid_in, norm_gain[l][None], mask, own_mask, w_in, w_mx, w_out, k_re[l], k_im[l], ft_mat,
            f_mat, *saved,
        )
        row_in = lax.psum_scatter(gw_in, "row", scatter_dimension=0, tiled=True)
        row_mix = lax.psum_scatter(gw_mix, "row", scatter_dimension=0, tiled=True)
        row_out = lax.psum_scatter(gw_out, "row", scatter_dimension=1, tiled=True)
        g_decay, g_b, g_c, g_row = params(dk, decay_t[l], step_t[l], b_t[l], c_t[l], sign, ft_mat)
        small = jnp.concatenate((in_sum[:, 0], mix_sum[:, 0], g_row[0], g_row[1]))
        big = jnp.stack((g_decay, g_b, g_c))
        small, big = lax.psum((small, big), "row")
        small = lax.all_gather(small, "dp", axis=0, tiled=False)
        big = big.reshape(3, states, 2, ch).transpose(0, 2, 3, 1)
        big = lax.all_gather(big, "dp", axis=2, tiled=True)
        norm_sums = lax.psum(norm_part, ("dp", "row", "col"))
        cuts = np.cumsum([0, ch, ch, hid, hid, ch, ch, ch, ch])
        parts = [small[:, cuts[i] : cuts[i + 1]].reshape(-1) for i in range(8)]
        outs.append((
            norm_sums[0], norm_sums[1],
            spread(row_in[:, :ch], 1), spread(row_in[:, ch:ch2], 1), spread(row_in[:, ch2:], 1),
            parts[0], parts[1], parts[2],
            big[0], jnp.stack((parts[4], parts[5])), big[1], big[2], jnp.stack((parts[6], parts[7])),
            spread(row_mix, 1), parts[3], spread(row_out, 0), norm_sums[2],
        ))
    ordered = outs[::-1]
    stacked = [jnp.stack([entry[i] for entry in ordered]) for i in range(17)]
    return (tokens_out, grad, *stacked)


def solution(mesh):
    tokens = P(("dp", "row", "col"), None)
    weight = P(None, "row", "col")
    bias = P(None, "col")
    state = P(None, None, "col", None)
    chan = P(None, None, "col")
    in_specs = (
        tokens, P(("dp", "row")), tokens, P(), P(), weight, weight, weight, bias, bias, bias,
        state, chan, state, state, chan, weight, bias, P(None, "col", "row"), P(),
    )
    out_specs = (
        tokens, tokens, P(), P(), weight, weight, weight, bias, bias, bias,
        state, chan, state, state, chan, weight, bias, P(None, "col", "row"), P(),
    )
    return jax.shard_map(body, mesh=mesh, in_specs=in_specs, out_specs=out_specs, check_vma=False)
```

time: 3040 us -> 868 us (0.29)
  matrix products: 1590 us -> 0 us
  local copies, waits for them, and re-layouts: 520 us -> 66 us
  Pallas kernels: 0 us -> 359 us
  other arithmetic: 379 us -> 24 us
  waiting for transfers between devices: 382 us -> 190 us
  blocking collectives: 127 us -> 206 us
    dot_general x54 -> x0, matrix products: 1590 us -> none  [the longest x12 591 us: ssm_scan(): carried = jnp.einsum('bcn,tcn->btc', block_starts, head, precision=HIGH)]
    pallas_call x0 -> x7, Pallas kernels: none -> 359 us  [the longest x2 169 us: body(): bwd(grad, resid_in, norm_gain[l][None], mask, own_mask, w_in, w_mx, w_out...]
    gather x8 -> x0, local copies, waits for them, and re-layouts: 166 us -> none  [ssm_scan(): jnp.take(kernel, lag_index, axis=0)]
    all_gather x4 -> x12, blocking collectives: 9.31 us -> 142 us  [the longest x8 88.3 us: spread(): return lax.all_gather(x, 'dp', axis=axis, tiled=True).astype(F32)]
    psum x2 -> x1, waiting for transfers between devices: 182 us -> 57.7 us  [body(): small, big = lax.psum((small, big), 'row')]
    scatter-add x4 -> x0, other arithmetic: 114 us -> none  [ssm_scan(): jnp.take(kernel, lag_index, axis=0)]
    dynamic_slice x49 -> x9, local copies, waits for them, and re-layouts: 108 us -> 1.34 us  [the longest x8 1.26 us: mine(): return lax.dynamic_slice_in_dim(x, d * size, size, axis)]
    all_gather x12 -> x8, waiting for transfers between devices: 171 us -> 74.9 us  [the longest x2 74.8 us: body(): big = lax.all_gather(big, 'dp', axis=2, tiled=True)]
  transfers between devices with their start and end apart: 26 -> 15, of which waited for: 10 -> 5; matrix products, arithmetic and copies ran while one was open for 60% -> 9% of each run, Pallas kernels for 0% -> 10%
where the time goes in v1:
time: 868 us; the launch traced here: 862 us
  Pallas kernels  359 us (41%)
  blocking collectives  206 us (24%)
  waiting for transfers between devices  190 us (22%)
  local copies, waits for them, and re-layouts  66 us (8%)
  other arithmetic  24 us (3%)
  between operations  15.8 us (2%)
    pallas_call x2, Pallas kernels, body(): bwd(grad, resid_in, norm_gain[l][None], mask, own_mask, w_in, w_mx, w_out...  169 us
    pallas_call x2, Pallas kernels, body(): fwd(residual, norm_gain[l][None], norm_shift[l][None], mask, own_mask, w_...  147 us
    all_gather x8, blocking collectives, spread(): return lax.all_gather(x, 'dp', axis=axis, tiled=True).astype(F32)  88.3 us
    all_gather x2, waiting for transfers between devices, body(): big = lax.all_gather(big, 'dp', axis=2, tiled=True)  74.8 us
    psum x1, waiting for transfers between devices, body(): small, big = lax.psum((small, big), 'row')  57.7 us
    psum x1, blocking collectives, body(): norm_sums = lax.psum(norm_part, ('dp', 'row', 'col'))  37.8 us
    all_gather x2, blocking collectives, body(): lax.all_gather(mine(w_output[l], hid, 0).astype(BF), 'row', axis=1, tiled...  37.6 us
    reduce_scatter x2, waiting for transfers between devices, body(): row_mix = lax.psum_scatter(gw_mix, 'row', scatter_dimension=0, tiled=True)  28.7 us
  transfers between devices with their start and end apart: 15, of which 5 were waited for; matrix products, arithmetic and copies ran while one was open for 9% of the time, Pallas kernels for 10%

profile of v1, /device:TPU:0, one launch (start us, length us, event | category | flops | bytes accessed | tf_op | source)
XLA Modules:
  0.0 862.4 jit_solution(6877366425749398511)
XLA Ops:
  7.3 1.4 fusion.17
  9.0 1.8 fusion.16
  11.8 2.7 fusion.12
  17.7 1.3 dynamic-slice_bitcast_fusion
  21.6 8.8 %all-reduce = s32[4]{0:T(128)S(1)} all-reduce(s32[4]{0:T(128)S(1)} %dynamic-update-slice), channel_id=1, replica_groups=mesh['dp'=4,'row'=4,'col'=2] {'dp'}, use_global_device_ids=true, to_apply=%add | all-reduce | flops 4 | bytes 32
  36.4 0.9 reshape.145.decay_ref
  39.3 0.9 broadcast_in_dim.35.in_bias_ref
  40.2 1.8 fusion.15
  42.0 17.9 %all-gather.1 = bf16[1,384,768]{1,2,0:T(8,128)(2,1)S(1)} all-gather(bf16[1,384,192]{1,2,0:T(8,128)(2,1)S(1)} %dynamic-slice_convert_fusion.4), channel_id=3, replica_groups=mesh['dp'=4,'row'=4,'col'=2] {'row'}, dimensions={2}, use_global_device_ids=true | all-gather | bytes 737280 | tf_op jit(solution)/shard_map/all_gather | solution.py:676
  60.0 0.9 broadcast_in_dim.34.in_bias_ref
  60.9 0.9 reshape.148.c_ref
  63.6 0.9 reshape.147.b_ref
  66.3 0.9 convert_element_type.58.res_ref
  67.1 0.9 convert_element_type.70.grad_ref
  68.0 1.1 copy.77
  69.1 19.7 %all-gather.3 = bf16[1,384,768]{1,2,0:T(8,128)(2,1)S(1)} all-gather(bf16[1,384,192]{1,2,0:T(8,128)(2,1)S(1)} %dynamic-slice_convert_fusion.2), channel_id=5, replica_groups=mesh['dp'=4,'row'=4,'col'=2] {'row'}, dimensions={2}, use_global_device_ids=true | all-gather | bytes 737280 | tf_op jit(solution)/shard_map/all_gather | solution.py:676
  88.8 1.1 copy.84
  90.6 17.5 %tables.1 = (f32[2,384,384]{2,1,0:T(8,128)}, f32[2,384,384]{2,1,0:T(8,128)}) custom-call(f32[2,64,384]{2,1,0:T(8,128)} %reshape.145.decay_ref, f32[2,1,384]{2,1,0:T(1,128)} %reshape.146.step_ref, f32[2,64,384]{2,1,0:T(8,128)} %reshape.147.b_ref, f32[2,64,384]{2,1,0:T(8,128)} %reshape.148.c_ref, f32[2,1,384]{2,1,0:T(1,128)} %reshape.149.skip_ref, ...), custom_call_target="tpu_custom_call" | custom-call | tf_op jit(solution)/shard_map/tables/pallas_call | solution.py:706
  110.0 2.3 slice_bitcast_fusion.1
  112.3 1.1 slice_bitcast_fusion
  113.4 70.4 %forward_block.2 = (f32[192,768]{1,0:T(8,128)}, bf16[1536,768]{1,0:T(8,128)(2,1)}, bf16[1536,1536]{1,0:T(8,128)(2,1)}, f32[4,768,384]{2,1,0:T(8,128)}, bf16[4,38...) custom-call(f32[192,768]{1,0:T(8,128)} %convert_element_type.58.res_ref, ...), custom_call_target="tpu_custom_call" | custom-call | tf_op jit(solution)/shard_map/forward_block/pallas_call | solution.py:775
  183.9 76.4 %forward_block.3 = (f32[192,768]{1,0:T(8,128)}, bf16[1536,768]{1,0:T(8,128)(2,1)}, bf16[1536,1536]{1,0:T(8,128)(2,1)}, f32[4,768,384]{2,1,0:T(8,128)}, bf16[4,38...) custom-call(f32[192,768]{1,0:T(8,128)} %get-tuple-element.63.res_ref, ...), custom_call_target="tpu_custom_call" | custom-call | tf_op jit(solution)/shard_map/forward_block/pallas_call | solution.py:775
  260.3 84.7 %backward_block.2 = (f32[192,768]{1,0:T(8,128)}, bf16[768,768]{1,0:T(8,128)(2,1)}, bf16[1536,384]{1,0:T(8,128)(2,1)}, bf16[384,768]{1,0:T(8,128)(2,1)}, f32[768,...) custom-call(f32[192,768]{1,0:T(8,128)} %convert_element_type.70.grad_ref, ...), custom_call_target="tpu_custom_call" | custom-call | tf_op jit(solution)/shard_map/backward_block/pallas_call | solution.py:806
  345.0 84.1 %backward_block.3 = (f32[192,768]{1,0:T(8,128)}, bf16[768,768]{1,0:T(8,128)(2,1)}, bf16[1536,384]{1,0:T(8,128)(2,1)}, bf16[384,768]{1,0:T(8,128)(2,1)}, f32[768,...) custom-call(f32[192,768]{1,0:T(8,128)} %get-tuple-element.72.grad_ref, ...), custom_call_target="tpu_custom_call" | custom-call | tf_op jit(solution)/shard_map/backward_block/pallas_call | solution.py:806
  429.2 13.1 %state_gradients.2 = (f32[64,384]{1,0:T(8,128)}, f32[64,384]{1,0:T(8,128)}, f32[64,384]{1,0:T(8,128)}, f32[8,384]{1,0:T(8,128)}) custom-call(f32[384,768]{1,0:T(8,128)} %get-tuple-element.87.dk_ref, f32[64,384]{1,0:T(8,128)} %squeeze.92.decay_ref, f32[1,384]{1,0:T(1,128)} %squeeze.93.step_ref, f32[64,384]{1,0:T(8,128)} %squeeze.94.b_ref, ...), custom_call_target="tpu_custom_call" | custom-call | tf_op jit(solution)/shard_map/state_gradients/pallas_call | solution.py:813
  442.3 1.0 pad_maximum_fusion.5
  443.6 13.2 %state_gradients.3 = (f32[64,384]{1,0:T(8,128)}, f32[64,384]{1,0:T(8,128)}, f32[64,384]{1,0:T(8,128)}, f32[8,384]{1,0:T(8,128)}) custom-call(f32[384,768]{1,0:T(8,128)} %get-tuple-element.91.dk_ref, f32[64,384]{1,0:T(8,128)} %squeeze.100.decay_ref, f32[1,384]{1,0:T(1,128)} %squeeze.101.step_ref, f32[64,384]{1,0:T(8,128)} %squeeze.102.b_ref, ...), custom_call_target="tpu_custom_call" | custom-call | tf_op jit(solution)/shard_map/state_gradients/pallas_call | solution.py:813
  456.8 1.0 pad_maximum_fusion.6
  458.1 1.2 copy.101
  459.3 1.2 copy.100
  461.1 1.1 copy.108
  462.3 1.1 copy.110
  464.7 57.7 %all-reduce.6.cloned.1.call-done = (f32[3,2,192,64]{3,1,0,2:T(2,128)}, f32[3,2,192,64]{3,1,0,2:T(2,128)}) async-done(((f32[3,2,192,64]{3,1,0,2:T(2,128)}, f32[3,2,192,64]{3,1,0,2:T(2,128)}), (f32[3,2,192,64]{3,1,0,2:T(2,128)}, f32[3,2,192,64]{3,1,0,2:T(2,128)})) %all-reduce.6.cloned.1.call-update) | async-done | bytes 589840 | tf_op jit(solution)/shard_map/psum | solution.py:816
  525.4 17.9 %all-reduce.2 = (f32[1,1920]{1,0:T(1,128)S(1)}, f32[1,1920]{1,0:T(1,128)S(1)}) all-reduce(f32[1,1920]{1,0:T(1,128)S(1)} %all_gather.84, f32[1,1920]{1,0:T(1,128)S(1)} %all_gather.82), channel_id=1, replica_groups=mesh['dp'=4,'row'=4,'col'=2] {'row'}, use_global_device_ids=true, to_apply=%region_5.6 | all-reduce | flops 3840 | bytes 30720 | tf_op jit(solution)/shard_map/psum | solution.py:816
  543.3 7.9 all-gather.4
  551.8 8.1 all-gather.5
  560.5 37.8 %all-reduce.1 = (f32[8,768]{1,0:T(8,128)S(1)}, f32[8,768]{1,0:T(8,128)S(1)}) all-reduce(f32[8,768]{1,0:T(8,128)S(1)} %copy-done.16, f32[8,768]{1,0:T(8,128)S(1)} %copy-done.17), channel_id=1, replica_groups=mesh['dp'=4,'row'=4,'col'=2] {'dp','row','col'}, use_global_device_ids=true, to_apply=%region_1.2 | all-reduce | flops 12288 | bytes 98304 | tf_op jit(solution)/shard_map/psum | solution.py:820
  604.8 1.0 copy.109
  605.9 1.0 copy.111
  607.0 12.2 %all_gather.90 = bf16[1536,192]{1,0:T(8,128)(2,1)S(1)} all-gather(bf16[384,192]{1,0:T(8,128)(2,1)S(1)} %copy.109), channel_id=1, replica_groups=mesh['dp'=4,'row'=4,'col'=2] {'dp'}, dimensions={0}, use_global_device_ids=true | all-gather | bytes 737280 | tf_op jit(solution)/shard_map/all_gather | solution.py:799
  619.1 10.9 %all_gather.91 = bf16[1536,192]{1,0:T(8,128)(2,1)S(1)} all-gather(bf16[384,192]{1,0:T(8,128)(2,1)S(1)} %copy.111), channel_id=1, replica_groups=mesh['dp'=4,'row'=4,'col'=2] {'dp'}, dimensions={0}, use_global_device_ids=true | all-gather | bytes 737280 | tf_op jit(solution)/shard_map/all_gather | solution.py:799
  630.5 2.4 copy.107
  632.9 1.1 fusion.20
  634.2 26.4 %reduce-scatter.11.cloned.1.call-done = bf16[192,768]{1,0:T(8,128)(2,1)} async-done(((bf16[768,768]{1,0:T(8,128)(2,1)}), bf16[192,768]{1,0:T(8,128)(2,1)}) %reduce-scatter.11.cloned.1.call-update) | async-done | bytes 294928 | tf_op jit(solution)/shard_map/reduce_scatter | solution.py:810
  660.5 1.1 fusion.19
  661.8 36.8 %all-gather.21.cloned.1.call-done = f32[3,2,768,64]{3,1,0,2:T(2,128)} async-done(((f32[3,2,192,64]{3,1,0,2:T(2,128)}), f32[3,2,768,64]{3,1,0,2:T(2,128)}) %all-gather.21.cloned.1.call-update) | async-done | bytes 1179664 | tf_op jit(solution)/shard_map/all_gather | solution.py:819
  698.6 2.6 fusion.14
  701.2 28.7 %reduce-scatter.17.cloned.1.call-done = bf16[384,384]{1,0:T(8,128)(2,1)} async-done(((bf16[1536,384]{1,0:T(8,128)(2,1)}), bf16[384,384]{1,0:T(8,128)(2,1)}) %reduce-scatter.17.cloned.1.call-update) | async-done | bytes 294928 | tf_op jit(solution)/shard_map/reduce_scatter | solution.py:811
  730.0 38.0 %all-gather.19.cloned.1.call-done = f32[3,2,768,64]{3,1,0,2:T(2,128)} async-done(((f32[3,2,192,64]{3,1,0,2:T(2,128)}), f32[3,2,768,64]{3,1,0,2:T(2,128)}) %all-gather.19.cloned.1.call-update) | async-done | bytes 1179664 | tf_op jit(solution)/shard_map/all_gather | solution.py:819
  768.0 3.0 fusion.13
  771.8 1.9 copy.106
  773.7 11.6 %all_gather.78 = bf16[192,768]{0,1:T(8,128)(2,1)S(1)} all-gather(bf16[192,192]{0,1:T(8,128)(2,1)S(1)} %copy.92), channel_id=1, replica_groups=mesh['dp'=4,'row'=4,'col'=2] {'dp'}, dimensions={1}, use_global_device_ids=true | all-gather | bytes 368640 | tf_op jit(solution)/shard_map/all_gather | solution.py:799
  785.3 10.8 %all_gather.79 = bf16[192,768]{0,1:T(8,128)(2,1)S(1)} all-gather(bf16[192,192]{0,1:T(8,128)(2,1)S(1)} %copy.93), channel_id=1, replica_groups=mesh['dp'=4,'row'=4,'col'=2] {'dp'}, dimensions={1}, use_global_device_ids=true | all-gather | bytes 368640 | tf_op jit(solution)/shard_map/all_gather | solution.py:799
  796.3 1.5 copy.103
  797.8 9.6 %all_gather.76 = bf16[192,768]{0,1:T(8,128)(2,1)S(1)} all-gather(bf16[192,192]{0,1:T(8,128)(2,1)S(1)} %copy.90), channel_id=1, replica_groups=mesh['dp'=4,'row'=4,'col'=2] {'dp'}, dimensions={1}, use_global_device_ids=true | all-gather | bytes 368640 | tf_op jit(solution)/shard_map/all_gather | solution.py:799
  807.4 9.9 %all_gather.77 = bf16[192,768]{0,1:T(8,128)(2,1)S(1)} all-gather(bf16[192,192]{0,1:T(8,128)(2,1)S(1)} %copy.91), channel_id=1, replica_groups=mesh['dp'=4,'row'=4,'col'=2] {'dp'}, dimensions={1}, use_global_device_ids=true | all-gather | bytes 368640 | tf_op jit(solution)/shard_map/all_gather | solution.py:799
  817.5 1.5 copy.102
  818.9 1.9 pad_maximum_fusion.1
  820.9 1.9 copy.105
  823.6 1.9 copy.104
  825.5 11.9 %all_gather.80 = bf16[192,1536]{1,0:T(8,128)(2,1)S(1)} all-gather(bf16[192,384]{1,0:T(8,128)(2,1)S(1)} %slice-done.1), channel_id=1, replica_groups=mesh['dp'=4,'row'=4,'col'=2] {'dp'}, dimensions={1}, use_global_device_ids=true | all-gather | bytes 737280 | tf_op jit(solution)/shard_map/all_gather | solution.py:799
  837.4 11.4 %all_gather.81 = bf16[192,1536]{1,0:T(8,128)(2,1)S(1)} all-gather(bf16[192,384]{1,0:T(8,128)(2,1)S(1)} %slice-done), channel_id=1, replica_groups=mesh['dp'=4,'row'=4,'col'=2] {'dp'}, dimensions={1}, use_global_device_ids=true | all-gather | bytes 737280 | tf_op jit(solution)/shard_map/all_gather | solution.py:799
  848.8 1.6 maximum_convert_fusion.2
  850.4 4.2 maximum_convert_fusion
  (216 shorter events, 37.4 us)
Async XLA Ops:
  7.2 10.1 %copy-start = (f32[2,2,768,64]{2,3,1,0:T(8,128)S(1)}, f32[2,2,768,64]{2,3,1,0:T(8,128)}, u32[]{:S(2)}) copy-start(f32[2,2,768,64]{2,3,1,0:T(8,128)} %param.33) | copy-start | bytes 2359300
  7.2 106.2 %all-gather.15.cloned.1.call-start = ((), (), s32[]{:S(2)}) async-start(), calls=%async_computation.6 | async-start | bytes 1474560 | tf_op jit(solution)/shard_map/all_gather | solution.py:674
  7.3 1.7 copy-start.13
  11.8 101.6 %all-gather.27.cloned.1.call-start = ((), (), s32[]{:S(2)}) async-start(), calls=%async_computation.16 | async-start | bytes 1474560 | tf_op jit(solution)/shard_map/all_gather | solution.py:675
  15.3 168.6 %all-gather.17.cloned.1.call-start = ((), (), s32[]{:S(2)}) async-start(), calls=%async_computation.7 | async-start | bytes 1474560 | tf_op jit(solution)/shard_map/all_gather | solution.py:674
  16.4 167.5 %all-gather.29.cloned.1.call-start = ((), (), s32[]{:S(2)}) async-start(), calls=%async_computation.17 | async-start | bytes 1474560 | tf_op jit(solution)/shard_map/all_gather | solution.py:675
  17.2 505.2 %all-reduce.6.cloned.1.call-start = ((), (), s32[]{:S(2)}) async-start(), calls=%async_computation.20 | async-start | bytes 2359296 | tf_op jit(solution)/shard_map/psum | solution.py:816
  17.7 2.5 copy-start.26
  17.7 12.7 %copy-start.25 = (f32[2,2,768]{2,1,0:T(2,128)S(1)}, f32[2,2,768]{2,1,0:T(2,128)}, u32[]{:S(2)}) copy-start(f32[2,2,768]{2,1,0:T(2,128)} %param.34) | copy-start | bytes 36868
  17.7 14.1 %copy-start.20 = (f32[2,768]{1,0:T(2,128)S(1)}, f32[2,768]{1,0:T(2,128)}, u32[]{:S(2)}) copy-start(f32[2,768]{1,0:T(2,128)} %param.30) | copy-start | bytes 18436
  17.7 14.1 %copy-start.21 = (f32[2,768]{1,0:T(2,128)S(1)}, f32[2,768]{1,0:T(2,128)}, u32[]{:S(2)}) copy-start(f32[2,768]{1,0:T(2,128)} %param.31) | copy-start | bytes 18436
  17.7 16.2 %copy-start.18 = (f32[2,1536]{1,0:T(2,128)S(1)}, f32[2,1536]{1,0:T(2,128)}, u32[]{:S(2)}) copy-start(f32[2,1536]{1,0:T(2,128)} %param.32) | copy-start | bytes 36868
  17.7 16.2 %copy-start.19 = (f32[2,1536]{1,0:T(2,128)S(1)}, f32[2,1536]{1,0:T(2,128)}, u32[]{:S(2)}) copy-start(f32[2,1536]{1,0:T(2,128)} %param.39) | copy-start | bytes 36868
  60.0 6.3 copy-start.11
  61.9 5.2 copy-start.12
  69.1 39.7 %copy-start.22 = (f32[2,768]{1,0:T(2,128)S(1)}, f32[2,768]{1,0:T(2,128)}, u32[]{:S(2)}) copy-start(f32[2,768]{1,0:T(2,128)} %param.25) | copy-start | bytes 18436
  88.8 20.6 %copy-start.23 = (f32[2,768]{1,0:T(2,128)S(1)}, f32[2,768]{1,0:T(2,128)}, u32[]{:S(2)}) copy-start(f32[2,768]{1,0:T(2,128)} %param.41) | copy-start | bytes 18436
  88.8 20.6 %copy-start.24 = (f32[2,768]{1,0:T(2,128)S(1)}, f32[2,768]{1,0:T(2,128)}, u32[]{:S(2)}) copy-start(f32[2,768]{1,0:T(2,128)} %param.26) | copy-start | bytes 18436
  108.1 4.2 copy-start.4
  459.3 1.8 copy-start.8
  460.5 1.8 copy-start.7
  460.5 141.7 %reduce-scatter.15.cloned.1.call-start = ((), (), s32[]{:S(2)}) async-start(), calls=%async_computation.12 | async-start | bytes 1474560 | tf_op jit(solution)/shard_map/reduce_scatter | solution.py:811
  461.1 143.8 %reduce-scatter.19.cloned.1.call-start = ((), (), s32[]{:S(2)}) async-start(), calls=%async_computation.18 | async-start | bytes 737280
  462.2 143.7 %reduce-scatter.21.cloned.1.call-start = ((), (), s32[]{:S(2)}) async-start(), calls=%async_computation.19 | async-start | bytes 737280
  463.3 169.5 %reduce-scatter.13.cloned.1.call-start = ((), (), s32[]{:S(2)}) async-start(), calls=%async_computation.9 | async-start | bytes 1474560 | tf_op jit(solution)/shard_map/reduce_scatter | solution.py:810
  464.1 59.0 %copy-start.15 = (f32[384,1]{1,0:T(8,128)S(1)}, f32[384,1]{1,0:T(8,128)}, u32[]{:S(2)}) copy-start(f32[384,1]{1,0:T(8,128)} %get-tuple-element.86) | copy-start | bytes 4612
  464.1 196.5 %reduce-scatter.11.cloned.1.call-start = ((), (), s32[]{:S(2)}) async-start(), calls=%async_computation.8 | async-start | bytes 1474560 | tf_op jit(solution)/shard_map/reduce_scatter | solution.py:810
  464.1 59.1 %copy-start.14 = (f32[384,1]{1,0:T(8,128)S(1)}, f32[384,1]{1,0:T(8,128)}, u32[]{:S(2)}) copy-start(f32[384,1]{1,0:T(8,128)} %get-tuple-element.90) | copy-start | bytes 4612
  464.1 59.2 %copy-start.10 = (f32[768,1]{1,0:T(8,128)S(1)}, f32[768,1]{1,0:T(8,128)}, u32[]{:S(2)}) copy-start(f32[768,1]{1,0:T(8,128)} %get-tuple-element.85) | copy-start | bytes 9220
  464.7 58.9 %copy-start.9 = (f32[768,1]{1,0:T(8,128)S(1)}, f32[768,1]{1,0:T(8,128)}, u32[]{:S(2)}) copy-start(f32[768,1]{1,0:T(8,128)} %get-tuple-element.89) | copy-start | bytes 9220
  464.7 233.9 %all-gather.21.cloned.1.call-start = ((), (), s32[]{:S(2)}) async-start(), calls=%async_computation.11 | async-start | bytes 2949120 | tf_op jit(solution)/shard_map/all_gather | solution.py:819
  522.4 38.1 %copy-start.16 = (f32[8,768]{1,0:T(8,128)S(1)}, f32[8,768]{1,0:T(8,128)}, u32[]{:S(2)}) copy-start(f32[8,768]{1,0:T(8,128)} %get-tuple-element.82) | copy-start | bytes 73732
  522.4 38.1 %copy-start.17 = (f32[8,768]{1,0:T(8,128)S(1)}, f32[8,768]{1,0:T(8,128)}, u32[]{:S(2)}) copy-start(f32[8,768]{1,0:T(8,128)} %get-tuple-element.81) | copy-start | bytes 73732
  522.4 207.5 %reduce-scatter.17.cloned.1.call-start = ((), (), s32[]{:S(2)}) async-start(), calls=%async_computation.14 | async-start | bytes 1474560 | tf_op jit(solution)/shard_map/reduce_scatter | solution.py:811
  523.0 79.8 %copy-start.6 = (f32[192,768]{1,0:T(8,128)S(1)}, f32[192,768]{1,0:T(8,128)}, u32[]{:S(2)}) copy-start(f32[192,768]{1,0:T(8,128)} %get-tuple-element.64) | copy-start | bytes 1769476
  523.0 245.0 %all-gather.19.cloned.1.call-start = ((), (), s32[]{:S(2)}) async-start(), calls=%async_computation.10 | async-start | bytes 2949120 | tf_op jit(solution)/shard_map/all_gather | solution.py:819
  598.4 252.0 %all-gather.23.cloned.1.call-start = ((), (), s32[]{:S(2)}) async-start(), calls=%async_computation.13 | async-start | bytes 1474560 | tf_op jit(solution)/shard_map/all_gather | solution.py:799
  602.2 248.2 %all-gather.25.cloned.1.call-start = ((), (), s32[]{:S(2)}) async-start(), calls=%async_computation.15 | async-start | bytes 1474560 | tf_op jit(solution)/shard_map/all_gather | solution.py:799
  768.0 3.0 copy-start.3
  820.9 1.9 copy-start.2
  823.6 1.9 slice-start.1
  823.6 13.8 %slice-start = ((bf16[192,768]{1,0:T(8,128)(2,1)}), bf16[192,384]{1,0:T(8,128)(2,1)S(1)}, s32[]{:S(2)}) async-start(bf16[192,768]{1,0:T(8,128)(2,1)} %reduce-scatter.13.cloned.1.call-done), calls=%async_computation.21 | async-start | bytes 294912 | tf_op jit(solution)/shard_map/slice | solution.py:825
  850.4 4.2 copy-start.5
  850.4 5.0 copy-start.1
Sparse Core Ops, SparseCore 0:
  11.9 33.1 all-gather.14
  46.7 37.2 all-gather.26
  85.6 29.8 all-gather.16
  116.9 29.5 all-gather.28
  460.6 61.7 all-reduce.5
  524.6 29.0 reduce-scatter.14
  556.5 20.6 reduce-scatter.18
  580.0 20.5 reduce-scatter.20
  602.9 27.5 reduce-scatter.12
  632.6 27.8 reduce-scatter.10
  662.4 36.1 all-gather.20
  700.8 29.1 reduce-scatter.16
  731.8 36.1 all-gather.18
  769.7 31.0 all-gather.22
  802.4 30.2 all-gather.24

commit v2 on v1

v2 whole, which is shorter than its diff:
```python
import functools

import jax
import jax.numpy as jnp
import numpy as np
from jax import lax
from jax.experimental import pallas as pl
from jax.experimental.pallas import tpu as pltpu
from jax.sharding import PartitionSpec as P

LAYERS = 2
EPS = 1e-05
LAG = 64
BF = jnp.bfloat16
F32 = jnp.float32
MESH = pl.DeviceIdType.MESH
VMEM_LIMIT = 60 * 1024 * 1024


def transform_matrix(length):
    k = np.arange(length)[:, None]
    t = np.arange(length)[None, :]
    angle = np.pi * (((2 * k + 1) * t) % (4 * length)) / (2 * length)
    return np.concatenate((np.cos(angle), -np.sin(angle)), axis=0)


def gelu_only(v):
    t = jnp.tanh(v * (0.7978845608 + 0.035677408 * v * v))
    return (0.5 * v) * (1.0 + t)


def gelu_parts(v):
    sq = v * v
    t = jnp.tanh(v * (0.7978845608 + 0.035677408 * sq))
    half = 0.5 + 0.5 * t
    slope = half + (v * half) * (1.0 - t) * (0.7978845608 + 0.107032225 * sq)
    return v * half, slope


def dot(a, b, ca, cb):
    return lax.dot_general(a, b, (((ca,), (cb,)), ((), ())), preferred_element_type=F32)


def over_rows(rows, step, work):
    def one(i, unused):
        work(pl.ds(pl.multiple_of(i * step, step), step))
        return unused

    lax.fori_loop(0, rows // step, one, 0)


def lane_sums(x):
    total = x[:, :128]
    for i in range(1, x.shape[1] // 128):
        total = total + x[:, 128 * i : 128 * (i + 1)]
    return total


def as_row(partial):
    return lax.dot_general(
        jnp.ones((8, 128), F32), partial, (((1,), (1,)), ((), ())), precision=lax.Precision.HIGHEST,
        preferred_element_type=F32,
    )


class Place:
    def __init__(self, n, m):
        self.n = n
        self.m = m
        self.d = lax.axis_index("dp")
        self.c = lax.axis_index("col")
        self.r = lax.axis_index("row")

    def greet(self):
        barrier = pltpu.get_barrier_semaphore()

        def hail(device):
            pl.semaphore_signal(barrier, inc=1, device_id=device, device_id_type=MESH)

        for k in range(1, self.n):
            hail({"dp": self.ahead(k)})
        hail({"col": 1 - self.c})

        def one(j, unused):
            hail({"row": self.up(j)})
            return unused

        lax.fori_loop(1, self.m, one, 0)
        pl.semaphore_wait(barrier, self.n + self.m - 1)

    def ahead(self, k):
        return lax.rem(self.d + k, self.n)

    def behind(self, k):
        return lax.rem(self.d - k + self.n, self.n)

    def up(self, j):
        return lax.rem(self.r + j, self.m)

    def down(self, j):
        return lax.rem(self.r - j + self.m, self.m)

    def other(self, i):
        return i + (i + self.n - self.d) // self.n

    def to_dp(self, src, dst, send, recv, q):
        return pltpu.make_async_remote_copy(
            src, dst, send, recv, device_id={"dp": q}, device_id_type=MESH
        )

    def to_mate(self, src, dst, send, recv):
        return pltpu.make_async_remote_copy(
            src, dst, send, recv, device_id={"col": 1 - self.c}, device_id_type=MESH
        )

    def to_row(self, src, dst, send, recv, q):
        return pltpu.make_async_remote_copy(
            src, dst, send, recv, device_id={"row": q}, device_id_type=MESH
        )


class RowSum:
    def __init__(self, place, part, got, send, recv):
        self.place, self.part, self.got, self.send, self.recv = place, part, got, send, recv

    def copy(self, j):
        q = self.place.up(j)
        return self.place.to_row(self.part.at[q], self.got.at[j], self.send.at[j], self.recv.at[j], q)

    def each(self, act):
        def one(j, unused):
            act(self.copy(j))
            return unused

        lax.fori_loop(1, self.place.m, one, 0)

    def start(self):
        self.each(lambda copy: copy.start())

    def total(self):
        self.each(lambda copy: copy.wait_recv())
        total = self.part[self.place.r].astype(F32)
        if self.place.m <= 4:
            for j in range(1, self.place.m):
                total = total + self.got[j].astype(F32)
            return total
        return lax.fori_loop(1, self.place.m, lambda j, t: t + self.got[j].astype(F32), total)

    def finish(self):
        self.each(lambda copy: copy.wait_send())


def gather_tokens(place, buf, rows, length, send_p, recv_p, send_m, recv_m):
    def region(slot):
        return buf.at[pl.ds(pl.multiple_of(slot * length + place.c * rows, rows), rows)]

    own = region(place.d)

    def peer(k):
        return place.to_dp(own, own, send_p.at[k], recv_p.at[k], place.ahead(k))

    def mate(k):
        part = region(place.behind(k))
        return place.to_mate(part, part, send_m.at[k], recv_m.at[k])

    def start():
        mate(0).start()
        for k in range(1, place.n):
            peer(k).start()

    def fetch(k):
        peer(k).wait_recv()
        forward = mate(k)
        forward.start()
        forward.wait_recv()

    def finish():
        def one(k, unused):
            peer(k).wait_send()
            mate(k).wait_send()
            return unused

        mate(0).wait_send()
        lax.fori_loop(1, place.n, one, 0)

    return start, lambda: mate(0).wait_recv(), fetch, finish


def norm_stats(residual):
    mean = jnp.mean(residual, axis=1, keepdims=True)
    centered = residual - mean
    variance = jnp.mean(centered * centered, axis=1, keepdims=True)
    inv = lax.rsqrt(variance + EPS)
    return centered * inv, inv


def sum_to_owner(place, rows, mate_out, mate_in, sum_out, sum_in, own, send_m, recv_m, send_p, recv_p):
    def to_mate(slot):
        return place.to_mate(mate_out.at[slot], mate_in.at[slot], send_m.at[slot], recv_m.at[slot])

    def to_owner(slot):
        k = lax.rem(slot - place.d + place.n, place.n)
        return place.to_dp(sum_out.at[slot], sum_in.at[k], send_p.at[k], recv_p.at[k], slot)

    def close(slot, mine):
        to_mate(slot).wait_recv()

        own[mine] = own[mine] + mate_in[slot].astype(F32)

        @pl.when(slot != place.d)
        def _():
            sum_out[slot] = own[mine].astype(BF)
            to_owner(slot).start()

    def receive():
        def one(k, unused):
            to_owner(place.ahead(k)).wait_recv()
            return unused

        lax.fori_loop(1, place.n, one, 0)

    def finish():
        def one(k, unused):
            to_owner(place.ahead(k)).wait_send()
            return unused

        lax.fori_loop(1, place.n, one, 0)

        def two(s, unused):
            to_mate(s).wait_send()
            return unused

        lax.fori_loop(0, place.n, two, 0)

    return to_mate, close, receive, finish


class RowGather:
    def __init__(self, place, shard, land, send, recv):
        self.place, self.shard, self.land, self.send, self.recv = place, shard, land, send, recv

    def copy(self, j):
        place = self.place
        return place.to_row(self.shard, self.land.at[place.r], self.send.at[j], self.recv.at[j], place.up(j))

    def each(self, act):
        def one(j, unused):
            act(self.copy(j))
            return unused

        lax.fori_loop(1, self.place.m, one, 0)

    def start(self):
        self.each(lambda copy: copy.start())
        self.land[self.place.r] = self.shard[...]

    def whole(self):
        self.each(lambda copy: copy.wait_recv())
        m, rows, lanes = self.land.shape
        return self.land[...].astype(F32).reshape(m * rows, lanes)

    def finish(self):
        self.each(lambda copy: copy.wait_send())


def kernel_spectrum(decay, step, b_in, c_out, skip, sign, ft_ref, rate, lead):
    length = ft_ref.shape[0]
    blocks = length // LAG
    rate[...] = jnp.exp(step) * jnp.exp(decay)
    weight = (1.0 - jnp.exp(-rate[...])) * jnp.exp(-decay) * b_in * c_out
    for b in range(blocks):
        lead[b] = weight * jnp.exp(-(LAG * b) * rate[...])
    lanes = rate.shape[1]
    offs = lax.broadcasted_iota(jnp.int32, (LAG, lanes), 0).astype(F32)

    def state(i, totals):
        powers = jnp.exp(-offs * rate[pl.ds(i, 1)])
        return tuple(totals[b] + powers * lead[b, pl.ds(i, 1)] for b in range(blocks))

    zero = jnp.zeros((LAG, lanes), F32)
    totals = list(lax.fori_loop(0, rate.shape[0], state, (zero,) * blocks, unroll=2))
    at_zero = lax.broadcasted_iota(jnp.int32, (LAG, lanes), 0) == 0
    totals[0] = totals[0] + jnp.where(at_zero, skip, 0.0)
    kernel = jnp.concatenate(totals, axis=0)
    k_hat = dot(kernel.T.astype(BF), ft_ref[...], 1, 0) * (1.0 / length)
    return k_hat[:, :length], k_hat[:, length:] * sign


def fwd_kernel(
    n, m, first, res_ref, gain_ref, shift_ref, own_live_ref, own_mask_ref, sh_mx, sh_out, in_bias_ref,
    mix_bias_ref, out_bias_ref, ft_ref, f_ref, decay_ref, step_ref, b_ref, c_ref, skip_ref, sign_ref, *rest
):
    if first:
        sh_in, sh_next, *rest = rest
    else:
        w_in_ref, *rest = rest
    new_ref, g_out, mx_out, pre_out, u_out, y_out, pm_out, prod_out, kre_out, kim_out, w_mx_out, w_out_out, *rest = rest
    if first:
        w_in_out, next_out, mask_ref, *rest = rest
    else:
        mask_ref = own_live_ref
    (
        w_in_t, w_mx_t, g, mx, pre, u_sp, y, pm, prod, act, spec, y_hat, prod_f, prod_t,
        kre_ref, kim_ref, rate, lead, land_mx, land_out, w_out_t,
        own, mate_out, mate_in, sum_out, sum_in,
        send_a, recv_a, send_am, recv_am, send_b, recv_b, send_bm, recv_bm, send_c, recv_c, send_cm, recv_cm, save,
        send_gm, recv_gm, send_go, recv_go, *rest,
    ) = rest
    place = Place(n, m)
    d, c = place.d, place.c
    rows, width = res_ref.shape
    length = ft_ref.shape[0]
    hid = sh_mx.shape[1]
    ch2 = decay_ref.shape[1]
    ch = ch2 // 2

    place.greet()
    gather_mx = RowGather(place, sh_mx, land_mx, send_gm, recv_gm)
    gather_out = RowGather(place, sh_out, land_out, send_go, recv_go)
    start_a, own_a, fetch_a, finish_a = gather_tokens(place, g, rows, length, send_a, recv_a, send_am, recv_am)
    if first:
        land_in, land_next, send_gi, recv_gi, send_gn, recv_gn, send_mk, recv_mk = rest
        gather_in = RowGather(place, sh_in, land_in, send_gi, recv_gi)
        gather_next = RowGather(place, sh_next, land_next, send_gn, recv_gn)
        gather_in.start()

        def mask_peer(k):
            return place.to_dp(
                own_live_ref, mask_ref.at[d], send_mk.at[k], recv_mk.at[k], place.ahead(k)
            )

        for k in range(1, n):
            mask_peer(k).start()
        mask_ref[d] = own_live_ref[...]
    else:
        gather_mx.start()
        gather_out.start()
    base = d * length + c * rows
    xhat, _ = norm_stats(res_ref[...])
    g[pl.ds(pl.multiple_of(base, rows), rows)] = (xhat * gain_ref[...] + shift_ref[...]).astype(BF)
    start_a()
    for j in range(ch2 // 128):
        at = slice(128 * j, 128 * (j + 1))
        kre_ref[at], kim_ref[at] = kernel_spectrum(
            decay_ref[:, at], step_ref[:, at], b_ref[:, at], c_ref[:, at], skip_ref[:, at], sign_ref[at], ft_ref,
            rate, lead,
        )
    kre_out[...] = kre_ref[...]
    kim_out[...] = kim_ref[...]
    if first:
        w_in = gather_in.whole()
        gather_mx.start()
        gather_out.start()
        w_in_out[...] = w_in.astype(BF)
        for k in range(1, n):
            mask_peer(k).wait_recv()
    else:
        w_in = w_in_ref[...].astype(F32)
    w_in_t[...] = w_in.T.astype(BF)
    own_a()

    def chunk(owner, slot):
        at = pl.ds(pl.multiple_of((c * n + owner) * ch, ch), ch)
        return mx.at[at, pl.ds(pl.multiple_of(slot * length, length), length)]

    def peer_b(k, slot):
        part = chunk(d, slot)
        return place.to_dp(part, part, send_b.at[slot, k], recv_b.at[slot, k], place.ahead(k))

    def mate_b(k, slot):
        part = chunk(place.behind(k), slot)
        return place.to_mate(part, part, send_bm.at[slot, k], recv_bm.at[slot, k])

    def saves(slot, item):
        lanes = pl.ds(pl.multiple_of(slot * length, length), length)
        src, dst = (
            lambda: (g.at[lanes], g_out.at[lanes]),
            lambda: (u_sp.at[slot], u_out.at[slot]),
            lambda: (y.at[slot], y_out.at[slot]),
            lambda: (pre.at[slot], pre_out.at[slot]),
            lambda: (mx.at[:, lanes], mx_out.at[:, lanes]),
            lambda: (pm.at[slot], pm_out.at[slot]),
            lambda: (prod.at[:, lanes], prod_out.at[:, lanes]),
        )[item]()
        return pltpu.make_async_copy(src, dst, save.at[item, slot])

    def scan_slot(i, unused):
        slot = lax.select(i == 0, d, place.other(i - 1))

        @pl.when(i > 0)
        def _():
            fetch_a(lax.rem(d - slot + n, n))

        lanes = pl.ds(pl.multiple_of(slot * length, length), length)
        pre[slot] = dot(w_in_t[...], g[lanes], 1, 1)
        live = mask_ref[slot, 0:1]
        v = pre[slot, :ch2] + in_bias_ref[:ch2]
        pre[slot, :ch2] = v
        act[...] = (gelu_only(v) * live).astype(BF)
        pre[slot, ch2:] = pre[slot, ch2:] + in_bias_ref[ch2:]
        spec[...] = dot(act[...], ft_ref[...], 1, 0)
        u_re, u_im = spec[:, :length], spec[:, length:]
        k_re, k_im = kre_ref[...], kim_ref[...]
        u_sp[slot, :, :length] = u_re.astype(BF)
        u_sp[slot, :, length:] = u_im.astype(BF)
        y_hat[:, :length] = (k_re * u_re - k_im * u_im).astype(BF)
        y_hat[:, length:] = (k_re * u_im + k_im * u_re).astype(BF)
        y[slot] = dot(y_hat[...], f_ref[...], 1, 0)
        mine = pl.ds(pl.multiple_of((c * n + d) * ch, ch), ch)
        mx[mine, lanes] = (y[slot, :ch] * y[slot, ch:]).astype(BF)
        mate_b(0, slot).start()
        for k in range(1, n):
            peer_b(k, slot).start()
        for item in range(4):
            saves(slot, item).start()
        return unused

    lax.fori_loop(0, n, scan_slot, 0)
    w_mx = gather_mx.whole()
    w_mx_out[...] = w_mx.astype(BF)
    w_mx_t[...] = w_mx.T.astype(BF)
    w_out = gather_out.whole()
    w_out_t[...] = w_out.astype(BF)
    w_out_out[...] = w_out.T.astype(BF)
    if first:
        gather_next.start()

    to_mate, close, receive, finish_c = sum_to_owner(
        place, rows, mate_out, mate_in, sum_out, sum_in, own, send_cm, recv_cm, send_c, recv_c
    )

    def order(i):
        return lax.select(i == n - 1, d, place.other(i))

    def hidden_slot(i, unused):
        slot = order(i)
        lanes = pl.ds(pl.multiple_of(slot * length, length), length)
        for k in range(1, n):
            peer_b(k, slot).wait_recv()
            mate_b(k, slot).start()
        for k in range(n):
            mate_b(k, slot).wait_recv()
        pm[slot] = dot(w_mx_t[...], mx[:, lanes], 1, 0)

        v = pm[slot] + mix_bias_ref[...]
        pm[slot] = v
        product = gelu_only(v) * gelu_only(pre[slot, ch2:])
        prod_f[...] = product
        prod[:, lanes] = product.astype(BF)
        prod_t[...] = prod_f[...].T.astype(BF)
        for item in range(4, 7):
            saves(slot, item).start()
        theirs = pl.ds(pl.multiple_of((1 - c) * rows, rows), rows)
        ours = pl.ds(pl.multiple_of(c * rows, rows), rows)
        mate_out[slot] = dot(prod_t[theirs], w_out_t[...], 1, 1).astype(BF)
        to_mate(slot).start()

        @pl.when(i > 0)
        def _():
            close(order(i - 1), lax.rem(i - 1, 2))

        own[lax.rem(i, 2)] = dot(prod_t[ours], w_out_t[...], 1, 1)
        return unused

    lax.fori_loop(0, n, hidden_slot, 0)
    last = (n - 1) % 2
    close(d, last)
    receive()

    total = own[last]
    for k in range(1, n):
        total = total + sum_in[k].astype(F32)
    new_ref[...] = res_ref[...] + own_mask_ref[...] * (total + out_bias_ref[...])
    finish_a()
    finish_c()
    gather_mx.finish()
    gather_out.finish()
    if first:
        next_out[...] = gather_next.whole().astype(BF)
        gather_next.finish()
        gather_in.finish()
        for k in range(1, n):
            mask_peer(k).wait_send()

    def drain(slot, unused):
        for k in range(1, n):
            peer_b(k, slot).wait_send()
        for k in range(n):
            mate_b(k, slot).wait_send()
        for item in range(7):
            saves(slot, item).wait()
        return unused

    lax.fori_loop(0, n, drain, 0)


def bwd_kernel(
    n, m, later, grad_ref, res_ref, gain_ref, mask_ref, own_mask_ref, w_in_ref, w_mx_ref, w_out_ref, kre_ref,
    kim_ref, ft_ref, f_ref, g_in, mx_in, pre_in, u_in, y_in, pm_in, prod_in, *rest
):
    if later:
        late_part, *rest = rest
    (new_ref, gw_in_ref, red_mx_ref, red_out_ref, in_row_ref, mix_row_ref, norm_sum_ref, dk_ref, *rest) = rest
    if later:
        red_late_ref, *rest = rest
    (
        gb, g, mx, pre, u_sp, y, pm, prod, gpre, gpre_f, gpm, gact, spec, hat, turned,
        mix_sum, mix_mate, mix_own, mix_got, in_sum, mix_acc, part_mx, got_mx, part_out, got_out,
        own, mate_out, mate_in, sum_out, sum_in,
        send_a, recv_a, send_am, recv_am, send_b, recv_b, send_bm, recv_bm, send_c, recv_c, send_cm, recv_cm, load,
        send_rm, recv_rm, send_ro, recv_ro, *rest,
    ) = rest
    place = Place(n, m)
    d, c = place.d, place.c
    rows, width = res_ref.shape
    length = ft_ref.shape[0]
    hid = w_mx_ref.shape[1]
    ch2 = kre_ref.shape[0]
    ch = ch2 // 2
    half = n * ch

    def loads(slot, item):
        lanes = pl.ds(pl.multiple_of(slot * length, length), length)
        src, dst = (
            lambda: (pre_in.at[slot], pre.at[slot]),
            lambda: (pm_in.at[slot], pm.at[slot]),
            lambda: (y_in.at[slot], y.at[slot]),
            lambda: (u_in.at[slot], u_sp.at[slot]),
            lambda: (prod_in.at[:, lanes], prod.at[:, lanes]),
            lambda: (mx_in.at[:, lanes], mx.at[:, lanes]),
            lambda: (g_in.at[lanes], g.at[lanes]),
        )[item]()
        return pltpu.make_async_copy(src, dst, load.at[item, slot])

    for item in range(7):
        loads(d, item).start()

    def start_loads(i, unused):
        for item in range(7):
            loads(place.other(i), item).start()
        return unused

    lax.fori_loop(0, n - 1, start_loads, 0)

    place.greet()
    start_a, own_a, fetch_a, finish_a = gather_tokens(place, gb, rows, length, send_a, recv_a, send_am, recv_am)
    base = d * length + c * rows
    first = grad_ref[...] * own_mask_ref[...]
    gb[pl.ds(pl.multiple_of(base, rows), rows)] = first.astype(BF)
    start_a()
    sum_mx = RowSum(place, part_mx, got_mx, send_rm, recv_rm)
    sum_out_w = RowSum(place, part_out, got_out, send_ro, recv_ro)
    row_sums = [sum_mx, sum_out_w]
    if later:
        got_late, send_rl, recv_rl = rest
        sum_late = RowSum(place, late_part, got_late, send_rl, recv_rl)
        sum_late.start()
        row_sums.append(sum_late)
    norm_sum_ref[...] = jnp.zeros_like(norm_sum_ref)
    norm_sum_ref[2:3] = jnp.sum(first, axis=0, keepdims=True)
    in_sum[...] = jnp.zeros_like(in_sum)
    mix_acc[...] = jnp.zeros_like(mix_acc)
    dk_ref[...] = jnp.zeros_like(dk_ref)
    own_a()

    def mate_b(slot):
        return place.to_mate(mix_sum.at[slot], mix_mate.at[slot], send_bm.at[slot], recv_bm.at[slot])

    def peer_b(k, slot):
        q = place.ahead(k)
        part = mix_sum.at[slot, pl.ds(pl.multiple_of(q * ch, ch), ch)]
        return place.to_dp(part, mix_got.at[k, slot], send_b.at[slot, k], recv_b.at[slot, k], q)

    def hidden_slot(i, unused):
        slot = lax.select(i == 0, d, place.other(i - 1))

        @pl.when(i > 0)
        def _():
            fetch_a(lax.rem(d - slot + n, n))

        lanes = pl.ds(pl.multiple_of(slot * length, length), length)
        gact[...] = dot(w_out_ref[...], gb[lanes], 1, 1)
        for item in range(2):
            loads(slot, item).wait()
        gated, slope = gelu_parts(pm[slot])
        value, value_slope = gelu_parts(pre[slot, ch2:])
        now = gact[...]
        to_value = now * gated * value_slope
        to_mix = now * value * slope
        gpre[ch2:, lanes] = to_value.astype(BF)
        gpm[:, lanes] = to_mix.astype(BF)
        in_sum[ch2:] = in_sum[ch2:] + lane_sums(to_value)
        mix_acc[...] = mix_acc[...] + lane_sums(to_mix)
        theirs = pl.ds(pl.multiple_of((1 - c) * half, half), half)
        ours = pl.ds(pl.multiple_of(c * half, half), half)
        mix_sum[slot] = dot(w_mx_ref[theirs], gpm[:, lanes], 1, 0).astype(BF)
        mate_b(slot).start()
        mix_own[...] = dot(w_mx_ref[ours], gpm[:, lanes], 1, 0)
        mate_b(slot).wait()
        mix_sum[slot] = (mix_own[...] + mix_mate[slot].astype(F32)).astype(BF)
        for k in range(1, n):
            peer_b(k, slot).start()
        return unused

    lax.fori_loop(0, n, hidden_slot, 0)

    def wait_loads(slot, unused):
        for item in range(2, 7):
            loads(slot, item).wait()
        return unused

    lax.fori_loop(0, n, wait_loads, 0)
    share = mx.shape[0] // m

    def grad_mix(q, unused):
        part_mx[q] = dot(mx[pl.ds(pl.multiple_of(q * share, share), share)], gpm[...], 1, 1).astype(BF)
        return unused

    lax.fori_loop(0, m, grad_mix, 0)
    sum_mx.start()
    gw_out = dot(prod[...], gb[...], 1, 0).T
    part_out[...] = gw_out.reshape(m, width // m, hid).astype(BF)
    sum_out_w.start()

    to_mate, close, receive, finish_c = sum_to_owner(
        place, rows, mate_out, mate_in, sum_out, sum_in, own, send_cm, recv_cm, send_c, recv_c
    )

    def order(i):
        return lax.select(i == n - 1, d, place.other(i))

    def scan_slot(i, unused):
        slot = order(i)
        lanes = pl.ds(pl.multiple_of(slot * length, length), length)
        for k in range(1, n):
            peer_b(k, slot).wait_recv()
        total = mix_sum[slot, pl.ds(pl.multiple_of(d * ch, ch), ch)].astype(F32)
        for k in range(1, n):
            total = total + mix_got[k, slot].astype(F32)
        hat[:ch, :length] = (total * y[slot, ch:]).astype(BF)
        hat[ch:, :length] = (total * y[slot, :ch]).astype(BF)
        spec[...] = dot(hat[:, :length], ft_ref[...], 1, 0)
        g_re, g_im = spec[:, :length], spec[:, length:]
        k_re, k_im = kre_ref[...], kim_ref[...]
        hat[:, :length] = (k_re * g_re + k_im * g_im).astype(BF)
        hat[:, length:] = (k_re * g_im - k_im * g_re).astype(BF)
        u_re, u_im = u_sp[slot, :, :length].astype(F32), u_sp[slot, :, length:].astype(F32)
        dk_ref[:, :length] = dk_ref[:, :length] + (u_re * g_re + u_im * g_im)
        dk_ref[:, length:] = dk_ref[:, length:] + (u_re * g_im - u_im * g_re)
        spec[:, :length] = dot(hat[...], f_ref[...], 1, 0)
        live = mask_ref[slot, 0:1]
        _, slope = gelu_parts(pre[slot, :ch2])
        part = spec[:, :length] * slope * live
        gpre_f[...] = part
        gpre[:ch2, lanes] = part.astype(BF)
        in_sum[:ch2] = in_sum[:ch2] + lane_sums(part)
        turned[:, :ch2] = gpre_f[...].T.astype(BF)
        gpre_f[...] = gpre[ch2:, lanes].astype(F32)
        turned[:, ch2:] = gpre_f[...].T.astype(BF)
        theirs = pl.ds(pl.multiple_of((1 - c) * rows, rows), rows)
        ours = pl.ds(pl.multiple_of(c * rows, rows), rows)
        mate_out[slot] = dot(turned[theirs], w_in_ref[...], 1, 1).astype(BF)
        to_mate(slot).start()

        @pl.when(i > 0)
        def _():
            close(order(i - 1), lax.rem(i - 1, 2))

        own[lax.rem(i, 2)] = dot(turned[ours], w_in_ref[...], 1, 1)
        return unused

    lax.fori_loop(0, n, scan_slot, 0)
    last = (n - 1) % 2
    close(d, last)

    def grad_in(r):
        part = dot(gpre[r], g[...], 1, 0).T
        gw_in_ref[:, :, r] = part.reshape(m, width // m, part.shape[1]).astype(BF)

    over_rows(gpre.shape[0], 128, grad_in)
    in_row_ref[...] = as_row(in_sum[...])
    mix_row_ref[...] = as_row(mix_acc[...])
    if later:
        red_late_ref[...] = sum_late.total().astype(BF)
    receive()
    total = own[last]
    for k in range(1, n):
        total = total + sum_in[k].astype(F32)
    xhat, inv = norm_stats(res_ref[...])
    h = total * gain_ref[...]
    middle = jnp.mean(h, axis=1, keepdims=True)
    along = jnp.mean(h * xhat, axis=1, keepdims=True)
    new_ref[...] = grad_ref[...] + inv * (h - middle - xhat * along)
    norm_sum_ref[0:1] = jnp.sum(total * xhat, axis=0, keepdims=True)
    norm_sum_ref[1:2] = jnp.sum(total, axis=0, keepdims=True)
    red_mx_ref[...] = sum_mx.total().astype(BF)
    red_out_ref[...] = sum_out_w.total().astype(BF)
    finish_a()
    finish_c()
    for row_sum in row_sums:
        row_sum.finish()

    def drain(slot, unused):
        for k in range(1, n):
            peer_b(k, slot).wait_send()
        return unused

    lax.fori_loop(0, n, drain, 0)


def state_grads(dk_re, dk_im, sign, ft_ref, decay, step, b_in, c_out, lag_sums):
    length = ft_ref.shape[0]
    re = dk_re.astype(BF)
    im = (dk_im * sign).astype(BF)
    lag_sums[...] = (dot(ft_ref[:, :length], re, 1, 1) + dot(ft_ref[:, length:], im, 1, 1)) * (1.0 / length)
    rate = jnp.exp(step) * jnp.exp(decay)
    a = jnp.exp(-rate)

    def lag(i, carry):
        total, slope = carry
        row = lag_sums[pl.ds(length - 1 - i, 1)]
        return total * a + row, slope * a + total

    zero = jnp.zeros_like(a)
    total, slope = lax.fori_loop(0, length, lag, (zero, zero), unroll=4)
    inv_decay = jnp.exp(-decay)
    gain = (1.0 - a) * inv_decay
    b_disc = gain * b_in
    to_b = c_out * total
    to_rate = a * (to_b * inv_decay * b_in - (c_out * b_disc) * slope)
    through = to_rate * rate
    return (
        through - to_b * b_disc, to_b * gain, b_disc * total,
        jnp.sum(through, axis=0, keepdims=True), lag_sums[0:1],
    )


def finish_kernel(
    n, m, part_in, late_in, red_mx0, red_out0, red_mx1, red_out1, dk0, dk1, in0, in1, mix0, mix1, norm0, norm1,
    decay_ref, step_ref, b_ref, c_ref, sign_ref, ft_ref,
    all_in, all_mx, all_out, all_states, all_small, norm_ref,
    got_in, red_in0, states, part_s, got_s, red_s, full_s, lag_sums, small, row_small, dp_small, norm_own, norm_got,
    send_w, recv_w, keep_w, send_ri, recv_ri, send_rs, recv_rs, send_gs, recv_gs, send_sm, recv_sm,
    send_ds, recv_ds, keep_s, send_n, recv_n, send_st, recv_st, keep_st,
):
    place = Place(n, m)
    d, r = place.d, place.r
    ch2 = decay_ref.shape[2]
    states_n = decay_ref.shape[1]
    place.greet()
    sum_in = RowSum(place, part_in, got_in, send_ri, recv_ri)
    sum_in.start()

    def spread(item, src, out, layer):
        def remote(k):
            return place.to_dp(
                src, out.at[layer, d], send_w.at[item, k], recv_w.at[item, k], place.ahead(k)
            )

        def local():
            return pltpu.make_async_copy(src, out.at[layer, d], keep_w.at[item])

        def start():
            for k in range(1, n):
                remote(k).start()
            local().start()

        def wait():
            for k in range(1, n):
                remote(k).wait_recv()
                remote(k).wait_send()
            local().wait()

        return start, wait

    spreads = [
        spread(0, red_mx1, all_mx, 1), spread(1, red_out1, all_out, 1), spread(2, late_in, all_in, 1),
        spread(3, red_mx0, all_mx, 0), spread(4, red_out0, all_out, 0), spread(5, red_in0, all_in, 0),
    ]
    for start, _ in spreads[:5]:
        start()

    small[...] = jnp.zeros_like(small)
    for l, (dk, in_row, mix_row, norm) in enumerate(((dk0, in0, mix0, norm0), (dk1, in1, mix1, norm1))):
        small[l, 0:1] = in_row[0:1]
        small[l, 1:2, :ch2] = mix_row[0:1]
        small[l, 3:6] = norm[0:3]
        length = ft_ref.shape[0]
        g_decay, g_b, g_c, g_step, g_skip = state_grads(
            dk[:, :length], dk[:, length:], sign_ref[...], ft_ref, decay_ref[l], step_ref[l], b_ref[l], c_ref[l],
            lag_sums,
        )
        small[l, 1:2, ch2:] = g_step
        small[l, 2:3, :ch2] = g_skip
        for i, part in enumerate((g_decay, g_b, g_c)):
            states[pl.ds((3 * l + i) * states_n, states_n)] = part
    share = states.shape[0] // m
    for q in range(m):
        part_s[q] = states[q * share : (q + 1) * share].astype(BF)
    sum_s = RowSum(place, part_s, got_s, send_rs, recv_rs)
    sum_s.start()
    row_small[r] = small[...]

    def small_row(j):
        return place.to_row(row_small.at[r], row_small.at[r], send_sm.at[j], recv_sm.at[j], place.up(j))

    def each(work, count):
        def one(j, unused):
            work(j)
            return unused

        lax.fori_loop(1, count, one, 0)

    each(lambda j: small_row(j).start(), m)

    red_s[...] = sum_s.total().astype(BF)
    full_s[r] = red_s[...]

    def state_row(j):
        return place.to_row(full_s.at[r], full_s.at[r], send_gs.at[j], recv_gs.at[j], place.up(j))

    each(lambda j: state_row(j).start(), m)
    each(lambda j: small_row(j).wait_recv(), m)
    total = row_small[0]
    for q in range(1, m):
        total = total + row_small[q]
    dp_small[d] = total

    def small_dp(k):
        return place.to_dp(dp_small.at[d], dp_small.at[d], send_ds.at[k], recv_ds.at[k], place.ahead(k))

    for k in range(1, n):
        small_dp(k).start()
    red_in0[...] = sum_in.total().astype(BF)
    spreads[5][0]()
    each(lambda j: state_row(j).wait_recv(), m)

    def states_dp(k):
        return place.to_dp(full_s, all_states.at[d], send_st.at[k], recv_st.at[k], place.ahead(k))

    keep_states = pltpu.make_async_copy(full_s, all_states.at[d], keep_st)
    keep_states.start()
    for k in range(1, n):
        states_dp(k).start()
    for k in range(1, n):
        small_dp(k).wait_recv()
    total = dp_small[0]
    for q in range(1, n):
        total = total + dp_small[q]
    norm_own[...] = total
    swap = place.to_mate(norm_own, norm_got, send_n, recv_n)
    swap.start()
    all_small[...] = dp_small[...]
    swap.wait_recv()
    norm_ref[...] = norm_own[...] + norm_got[...]
    swap.wait_send()
    for _, wait in spreads:
        wait()
    for k in range(1, n):
        states_dp(k).wait_recv()
        states_dp(k).wait_send()
        small_dp(k).wait_send()
    keep_states.wait()
    each(lambda j: small_row(j).wait_send(), m)
    each(lambda j: state_row(j).wait_send(), m)
    sum_in.finish()
    sum_s.finish()


VM = pl.BlockSpec(memory_space=pltpu.VMEM)
ANY = pl.BlockSpec(memory_space=pl.ANY)


def shape(dims, dtype):
    return jax.ShapeDtypeStruct(tuple(dims), dtype)


def sem(*dims):
    return pltpu.SemaphoreType.DMA(dims)


def body(
    tokens_in, lengths, cotangent, norm_gain, norm_shift, w_fwd, w_bwd, w_value, bias_fwd, bias_bwd,
    bias_value, decay_log, step_log, b_input, c_output, skip_gain, w_mix, bias_mix, w_output, bias_output,
):
    n = lax.axis_size("dp")
    m = lax.axis_size("row")
    cols = lax.axis_size("col")
    d = lax.axis_index("dp")
    rows, width = tokens_in.shape
    length = rows * cols
    ch = w_fwd.shape[2] // n
    ch2 = 2 * ch
    hid = w_mix.shape[2] // n
    wide = ch2 + hid
    chans = n * cols * ch
    tokens = n * length
    matrix = transform_matrix(length)
    f_mat = jnp.asarray(matrix, BF)
    ft_mat = jnp.asarray(np.ascontiguousarray(matrix.T), BF)

    def mine(x, size, axis):
        return lax.dynamic_slice_in_dim(x, d * size, size, axis)

    shards, biases = [], []
    for l in range(LAYERS):
        shards.append((
            jnp.concatenate(
                (mine(w_fwd[l], ch, 1), mine(w_bwd[l], ch, 1), mine(w_value[l], hid, 1)), axis=1
            ).astype(BF),
            mine(w_mix[l], hid, 1).astype(BF),
            mine(w_output[l], hid, 0).astype(BF).T,
        ))
        in_bias = jnp.concatenate(
            (mine(bias_fwd[l], ch, 0), mine(bias_bwd[l], ch, 0), mine(bias_value[l], hid, 0))
        )[:, None]
        biases.append((in_bias, mine(bias_mix[l], hid, 0)[:, None], bias_output[l][None]))

    positions = jnp.arange(length, dtype=jnp.int32)
    live = (positions < lengths[0]).astype(F32)
    own_live = jnp.broadcast_to(live[None], (8, length))
    own_mask = lax.dynamic_slice_in_dim(live, lax.axis_index("col") * rows, rows, 0)[:, None]

    def states_first(x):
        part = mine(x, ch, 2)
        return part.transpose(0, 3, 1, 2).reshape(LAYERS, x.shape[3], ch2)

    def one_row(x):
        return mine(x, ch, 2).reshape(LAYERS, 1, ch2)

    decay_t, b_t, c_t = states_first(decay_log), states_first(b_input), states_first(c_output)
    step_t, skip_t = one_row(step_log), one_row(skip_gain)
    states = decay_t.shape[1]
    sign = jnp.where(jnp.arange(ch2) < ch, 1.0, -1.0).astype(F32)[:, None]
    comm = [
        sem(n), sem(n), sem(n), sem(n), sem(n, n), sem(n, n),
    ]
    sums = [
        pltpu.VMEM((2, rows, width), F32), pltpu.VMEM((n, rows, width), BF), pltpu.VMEM((n, rows, width), BF),
        pltpu.VMEM((n, rows, width), BF), pltpu.VMEM((n, rows, width), BF),
    ]
    saved_shapes = (
        shape((tokens, width), BF), shape((chans, tokens), BF), shape((n, wide, length), F32),
        shape((n, ch2, 2 * length), BF), shape((n, ch2, length), F32), shape((n, hid, length), F32),
        shape((hid, tokens), BF),
    )
    def fwd(first):
        table = shape((ch2, length), F32)
        ahead = shape((width, wide), BF)
        extra = (ahead, ahead, shape((n, 8, length), F32)) if first else ()
        lands = [(m, chans // m, hid), (m, width // m, hid)]
        return pl.pallas_call(
            functools.partial(fwd_kernel, n, m, first),
            out_shape=(
                shape((rows, width), F32), *saved_shapes, table, table, shape((chans, hid), BF),
                shape((hid, width), BF), *extra,
            ),
            in_specs=[VM] * (18 + 1 + first),
            out_specs=(VM, *([ANY] * 7), *([VM] * (4 + len(extra)))),
            scratch_shapes=[
                pltpu.VMEM((wide, width), BF), pltpu.VMEM((hid, chans), BF),
                *(pltpu.VMEM(s.shape, s.dtype) for s in saved_shapes),
                pltpu.VMEM((ch2, length), BF), pltpu.VMEM((ch2, 2 * length), F32),
                pltpu.VMEM((ch2, 2 * length), BF), pltpu.VMEM((hid, length), F32), pltpu.VMEM((length, hid), BF),
                pltpu.VMEM((ch2, length), F32), pltpu.VMEM((ch2, length), F32),
                pltpu.VMEM((states, 128), F32), pltpu.VMEM((length // LAG, states, 128), F32),
                *(pltpu.VMEM(s, BF) for s in lands), pltpu.VMEM((width, hid), BF),
                *sums, *comm, sem(n, n), sem(n, n), sem(n), sem(n), sem(n), sem(n), sem(7, n),
                sem(m), sem(m), sem(m), sem(m),
                *([pltpu.VMEM((m, width // m, wide), BF)] * 2 + [sem(m)] * 4 + [sem(n)] * 2 if first else []),
            ],
            compiler_params=pltpu.CompilerParams(
                collective_id=4 if first else 0, has_side_effects=True, vmem_limit_bytes=VMEM_LIMIT
            ),
            name="forward_block",
        )

    def bwd(later):
        late = (m, width // m, wide)
        out_shape = [
            shape((rows, width), F32), shape(late, BF), shape((chans // m, hid), BF), shape((width // m, hid), BF),
            shape((8, wide), F32), shape((8, hid), F32), shape((8, width), F32), shape((ch2, 2 * length), F32),
        ]
        if later:
            out_shape.append(shape(late[1:], BF))
        return pl.pallas_call(
            functools.partial(bwd_kernel, n, m, later),
            out_shape=tuple(out_shape),
            in_specs=[VM] * 12 + [ANY] * 7 + [VM] * later,
            out_specs=(VM,) * len(out_shape),
            scratch_shapes=[
                pltpu.VMEM((tokens, width), BF),
                *(pltpu.VMEM(s.shape, s.dtype) for s in saved_shapes),
                pltpu.VMEM((wide, tokens), BF), pltpu.VMEM((ch2, length), F32), pltpu.VMEM((hid, tokens), BF),
                pltpu.VMEM((hid, length), F32), pltpu.VMEM((ch2, 2 * length), F32),
                pltpu.VMEM((ch2, 2 * length), BF), pltpu.VMEM((length, wide), BF),
                pltpu.VMEM((n, n * ch, length), BF), pltpu.VMEM((n, n * ch, length), BF),
                pltpu.VMEM((n * ch, length), F32),
                pltpu.VMEM((n, n, ch, length), BF), pltpu.VMEM((wide, 128), F32), pltpu.VMEM((hid, 128), F32),
                *(pltpu.VMEM((m, chans // m, hid), BF),) * 2, *(pltpu.VMEM((m, width // m, hid), BF),) * 2,
                *sums, *comm, sem(n), sem(n), sem(n), sem(n), sem(n), sem(n), sem(7, n),
                sem(m), sem(m), sem(m), sem(m),
                *([pltpu.VMEM(late, BF), sem(m), sem(m)] if later else []),
            ],
            compiler_params=pltpu.CompilerParams(
                collective_id=1 + later, has_side_effects=True, vmem_limit_bytes=VMEM_LIMIT
            ),
            name="backward_block",
        )

    residual = tokens_in.astype(F32)
    stored = []
    for l in range(LAYERS):
        sh_in, sh_mx, sh_out = shards[l]
        first = l == 0
        given = (sh_in, shards[1][0]) if first else (w_next,)
        new, *made = fwd(first)(
            residual, norm_gain[l][None], norm_shift[l][None], own_live if first else mask, own_mask, sh_mx, sh_out,
            *biases[l], ft_mat, f_mat, decay_t[l], step_t[l], b_t[l], c_t[l], skip_t[l], sign, *given,
        )
        saved, (kre, kim, w_mx, w_out) = made[:7], made[7:11]
        if first:
            w_in, w_next, mask = made[11:]
        else:
            w_in = w_next
        stored.append((residual, saved, kre, kim, w_in, w_mx, w_out))
        residual = new
    tokens_out = residual.astype(BF)

    grad = cotangent.astype(F32)
    parts = [None] * LAYERS
    extra = ()
    for l in reversed(range(LAYERS)):
        resid_in, saved, kre, kim, w_in, w_mx, w_out = stored[l]
        grad, *parts[l] = bwd(l < LAYERS - 1)(
            grad, resid_in, norm_gain[l][None], mask, own_mask, w_in, w_mx, w_out, kre, kim, ft_mat,
            f_mat, *saved, *extra,
        )
        extra = (parts[l][0],)
    part_in, red_mx0, red_out0, in0, mix0, norm0, dk0, late_in = parts[0]
    _, red_mx1, red_out1, in1, mix1, norm1, dk1 = parts[1]
    lots = LAYERS * 3 * states
    all_in, all_mx, all_out, all_states, all_small, norms = pl.pallas_call(
        functools.partial(finish_kernel, n, m),
        out_shape=(
            shape((LAYERS, n, width // m, wide), BF), shape((LAYERS, n, chans // m, hid), BF),
            shape((LAYERS, n, width // m, hid), BF), shape((n, m, lots // m, ch2), BF),
            shape((n, LAYERS, 8, wide), F32), shape((LAYERS, 8, wide), F32),
        ),
        in_specs=[VM] * 20,
        out_specs=(ANY, ANY, ANY, ANY, VM, VM),
        scratch_shapes=[
            pltpu.VMEM((m, width // m, wide), BF), pltpu.VMEM((width // m, wide), BF), pltpu.VMEM((lots, ch2), F32),
            pltpu.VMEM((m, lots // m, ch2), BF), pltpu.VMEM((m, lots // m, ch2), BF),
            pltpu.VMEM((lots // m, ch2), BF), pltpu.VMEM((m, lots // m, ch2), BF), pltpu.VMEM((length, ch2), F32),
            pltpu.VMEM((LAYERS, 8, wide), F32), pltpu.VMEM((m, LAYERS, 8, wide), F32),
            pltpu.VMEM((n, LAYERS, 8, wide), F32), pltpu.VMEM((LAYERS, 8, wide), F32),
            pltpu.VMEM((LAYERS, 8, wide), F32),
            sem(6, n), sem(6, n), sem(6), sem(m), sem(m), sem(m), sem(m), sem(m), sem(m), sem(m), sem(m),
            sem(n), sem(n), sem(1), pltpu.SemaphoreType.DMA, pltpu.SemaphoreType.DMA, sem(n), sem(n),
            pltpu.SemaphoreType.DMA,
        ],
        compiler_params=pltpu.CompilerParams(
            collective_id=3, has_side_effects=True, vmem_limit_bytes=VMEM_LIMIT
        ),
        name="finish",
    )(
        part_in, late_in, red_mx0, red_out0, red_mx1, red_out1, dk0, dk1, in0, in1, mix0, mix1, norm0, norm1,
        decay_t, step_t, b_t, c_t, sign, ft_mat,
    )

    def columns(x):
        x = x.transpose(0, 2, 1, 3)
        return x.reshape(x.shape[0], x.shape[1], -1).astype(F32)

    def along(x):
        return x.transpose(1, 0, 2).reshape(LAYERS, -1)

    by_state = all_states.reshape(n, LAYERS, 3, states, 2, ch)
    by_state = by_state.transpose(2, 1, 4, 0, 5, 3).reshape(3, LAYERS, 2, n * ch, states).astype(F32)

    def per_direction(x):
        return x.reshape(n, LAYERS, 2, ch).transpose(1, 2, 0, 3).reshape(LAYERS, 2, n * ch)

    return (
        tokens_out, grad, norms[:, 3], norms[:, 4],
        columns(all_in[..., :ch]), columns(all_in[..., ch:ch2]), columns(all_in[..., ch2:]),
        along(all_small[:, :, 0, :ch]), along(all_small[:, :, 0, ch:ch2]), along(all_small[:, :, 0, ch2:]),
        by_state[0], per_direction(all_small[:, :, 1, ch2:]), by_state[1], by_state[2],
        per_direction(all_small[:, :, 2, :ch2]), columns(all_mx), along(all_small[:, :, 1, :hid]),
        all_out.transpose(0, 1, 3, 2).reshape(LAYERS, n * hid, width // m).astype(F32), norms[:, 5],
    )


def solution(mesh):
    tokens = P(("dp", "row", "col"), None)
    weight = P(None, "row", "col")
    bias = P(None, "col")
    state = P(None, None, "col", None)
    chan = P(None, None, "col")
    in_specs = (
        tokens, P(("dp", "row")), tokens, P(), P(), weight, weight, weight, bias, bias, bias,
        state, chan, state, state, chan, weight, bias, P(None, "col", "row"), P(),
    )
    out_specs = (
        tokens, tokens, P(), P(), weight, weight, weight, bias, bias, bias,
        state, chan, state, state, chan, weight, bias, P(None, "col", "row"), P(),
    )
    return jax.shard_map(body, mesh=mesh, in_specs=in_specs, out_specs=out_specs, check_vma=False)
```

time: 868 us -> 527 us (0.61)
  blocking collectives: 206 us -> 0 us
  waiting for transfers between devices: 190 us -> 0 us
  Pallas kernels: 359 us -> 424 us
  local copies, waits for them, and re-layouts: 66 us -> 83.8 us
  between operations: 15.8 us -> 2.14 us
  other arithmetic: 24 us -> 12.2 us
    all_gather x12 -> x0, blocking collectives: 142 us -> none  [the longest x8 88.3 us: spread(): return lax.all_gather(x, 'dp', axis=axis, tiled=True).astype(F32)]
    all_gather x8 -> x0, waiting for transfers between devices: 74.9 us -> none  [the longest x2 74.8 us: body(): big = lax.all_gather(big, 'dp', axis=2, tiled=True)]
    pallas_call x7 -> x5, Pallas kernels: 359 us -> 424 us  [the longest x2 170 us: body(): fwd(first)]
    psum x1 -> x0, waiting for transfers between devices: 57.7 us -> none  [body(): small, big = lax.psum((small, big), 'row')]
    psum x2 -> x0, blocking collectives: 55.7 us -> none  [the longest x1 37.8 us: body(): norm_sums = lax.psum(norm_part, ('dp', 'row', 'col'))]
    reduce_scatter x4 -> x0, waiting for transfers between devices: 55.1 us -> none  [the longest x2 28.7 us: body(): row_mix = lax.psum_scatter(gw_mix, 'row', scatter_dimension=0, tiled=True)]
    convert_element_type x2 -> x8, local copies, waits for them, and re-layouts: 0.04 us -> 25.1 us  [the longest x6 18.4 us: columns(): return x.reshape(x.shape[0], x.shape[1], -1).astype(F32)]
    another operation x23 -> x0, other arithmetic: 17.7 us -> none  [the longest x21 15.7 us: body(): stacked = [jnp.stack([entry[i] for entry in ordered]) for i in range(17)]]
  transfers between devices with their start and end apart: 15 -> 0, of which waited for: 5 -> 0; matrix products, arithmetic and copies ran while one was open for 9% -> 0% of each run, Pallas kernels for 10% -> 0%
where the time goes in v2:
time: 527 us; the launch traced here: 522 us
  Pallas kernels  424 us (80%)
  local copies, waits for them, and re-layouts  83.8 us (16%)
  other arithmetic  12.2 us (2%)
    pallas_call x2, Pallas kernels, body(): fwd(first)  170 us
    pallas_call x2, Pallas kernels, body(): bwd(l < LAYERS - 1)  163 us
    pallas_call x1, Pallas kernels, body(): pl.pallas_call(functools.partial(finish_kernel, n, m), out_shape=(shape((...  90.5 us
    convert_element_type x6, local copies, waits for them, and re-layouts, columns(): return x.reshape(x.shape[0], x.shape[1], -1).astype(F32)  18.4 us
    unnamed x33, local copies, waits for them, and re-layouts  11 us

profile of v2, /device:TPU:0, one launch (start us, length us, event | category | flops | bytes accessed | tf_op | source)
XLA Modules:
  0.0 522.1 jit_solution(4394442173752026956)
XLA Ops:
  1.5 0.8 constant_dynamic-slice_fusion.8
  2.9 1.4 fusion.33
  4.3 0.8 fusion.30
  5.1 0.8 fusion.31
  6.0 0.8 constant_dynamic-slice_fusion
  9.9 1.4 fusion.29
  11.3 0.8 fusion.28
  12.1 0.8 fusion.27
  13.1 0.8 copy.58.own_mask_ref
  13.9 0.7 fusion.2.sign_ref
  14.6 0.8 copy.60.mix_bias_ref
  15.4 0.8 copy.66.mix_bias_ref
  16.6 0.9 reshape.160.decay_ref
  17.6 0.8 squeeze.87.decay_ref
  18.5 0.8 squeeze.82.decay_ref
  19.3 0.9 broadcast_in_dim.38.in_bias_ref
  20.2 0.9 broadcast_in_dim.39.in_bias_ref
  21.1 1.3 dynamic-slice_bitcast_fusion
  22.6 0.9 reshape.163.c_ref
  23.6 0.8 squeeze.90.c_ref
  24.5 0.8 squeeze.85.c_ref
  25.5 0.9 reshape.162.b_ref
  26.5 0.8 squeeze.89.b_ref
  27.4 0.8 squeeze.84.b_ref
  28.2 0.9 convert_element_type.95.res_ref
  29.0 0.9 convert_element_type.106.grad_ref
  29.9 1.3 fusion.21
  31.7 0.8 pad_maximum_fusion.rest_0_
  32.6 0.8 pad_maximum_fusion.1.rest_1_
  33.5 0.8 fusion.3
  34.8 0.9 fusion
  35.7 96.6 %forward_block.2 = (f32[192,768]{1,0:T(8,128)}, bf16[1536,768]{1,0:T(8,128)(2,1)}, bf16[1536,1536]{1,0:T(8,128)(2,1)}, f32[4,768,384]{2,1,0:T(8,128)}, bf16[4,38...) custom-call(f32[192,768]{1,0:T(8,128)} %convert_element_type.95.res_, ...), custom_call_target="tpu_custom_call" | custom-call | tf_op jit(solution)/shard_map/forward_block/pallas_call | solution.py:1017
  132.2 73.6 %forward_block.3 = (f32[192,768]{1,0:T(8,128)}, bf16[1536,768]{1,0:T(8,128)(2,1)}, bf16[1536,1536]{1,0:T(8,128)(2,1)}, f32[4,768,384]{2,1,0:T(8,128)}, bf16[4,38...) custom-call(f32[192,768]{1,0:T(8,128)} %get-tuple-element.69.res_ref, ...), custom_call_target="tpu_custom_call" | custom-call | tf_op jit(solution)/shard_map/forward_block/pallas_call | solution.py:1017
  205.8 1.8 convert_element_type.105
  207.6 83.5 %backward_block.2 = (f32[192,768]{1,0:T(8,128)}, bf16[4,192,768]{2,1,0:T(8,128)(2,1)}, bf16[384,384]{1,0:T(8,128)(2,1)}, bf16[192,384]{1,0:T(8,128)(2,1)}, f32[8...) custom-call(f32[192,768]{1,0:T(8,128)} %convert_element_type.106.grad_ref, ...), custom_call_target="tpu_custom_call" | custom-call | tf_op jit(solution)/shard_map/backward_block/pallas_call | solution.py:1035
  291.2 79.8 %backward_block.3 = (f32[192,768]{1,0:T(8,128)}, bf16[4,192,768]{2,1,0:T(8,128)(2,1)}, bf16[384,384]{1,0:T(8,128)(2,1)}, bf16[192,384]{1,0:T(8,128)(2,1)}, f32[8...) custom-call(f32[192,768]{1,0:T(8,128)} %get-tuple-element.84.grad_ref, ...), custom_call_target="tpu_custom_call" | custom-call | tf_op jit(solution)/shard_map/backward_block/pallas_call | solution.py:1035
  371.0 90.5 %finish.1 = (bf16[2,4,192,768]{3,2,1,0:T(8,128)(2,1)}, bf16[2,4,384,384]{3,2,1,0:T(8,128)(2,1)}, bf16[2,4,192,384]{3,2,1,0:T(8,128)(2,1)}, bf16[4,4,96,384]{3,2,...) custom-call(bf16[4,192,768]{2,1,0:T(8,128)(2,1)} %get-tuple-element.99.part_in, ...), custom_call_target="tpu_custom_call" | custom-call | tf_op jit(solution)/shard_map/finish/pallas_call | solution.py:1043
  461.5 0.9 fusion.26
  464.2 1.0 fusion.25
  465.2 1.1 slice_reduce_fusion
  466.4 0.7 reshape.165
  467.2 0.7 reshape.168
  467.9 0.7 reshape.164
  469.9 0.7 reshape.167
  470.6 1.4 convert_bitcast_fusion.1
  472.0 1.7 copy.93
  473.7 0.8 copy-done.2
  474.7 1.7 copy.92
  476.8 2.2 copy.73
  479.0 3.0 reshape.171
  482.0 2.2 copy.72
  484.2 3.3 reshape.170
  487.5 5.0 reshape.175
  492.4 4.2 fusion.17
  496.6 0.7 copy.80
  497.2 1.6 squeeze.99
  498.8 1.9 copy.79
  500.7 1.6 squeeze.98
  502.2 0.7 copy.77
  502.9 1.6 squeeze.97
  504.5 4.2 convert_bitcast_fusion
  508.6 6.1 %copy.82 = f32[2,384,4,384]{1,3,2,0:T(8,128)} copy(f32[2,384,4,384]{3,1,2,0:T(8,128)} %convert_bitcast_fusion) | data formatting | bytes 9437184 | tf_op jit(solution)/shard_map/convert_element_type | solution.py:1074
  514.7 6.2 %copy.84 = f32[2,384,1536]{2,1,0:T(8,128)} copy(f32[2,384,1536]{1,2,0:T(8,128)} %bitcast.96) | data formatting | bytes 9437184
  520.9 0.8 copy.106
  (73 shorter events, 10.6 us)
Async XLA Ops:
  0.7 15.6 %copy-start = (f32[2,2,768,64]{2,3,1,0:T(8,128)S(1)}, f32[2,2,768,64]{2,3,1,0:T(8,128)}, u32[]{:S(2)}) copy-start(f32[2,2,768,64]{2,3,1,0:T(8,128)} %param.33) | copy-start | bytes 2359300
  22.6 5.6 %copy-start.7 = (bf16[192,768]{1,0:T(8,128)(2,1)S(1)}, bf16[192,768]{1,0:T(8,128)(2,1)}, u32[]{:S(2)}) copy-start(bf16[192,768]{1,0:T(8,128)(2,1)} %param.22) | copy-start | bytes 884740
  23.5 5.5 %copy-start.8 = (bf16[192,768]{1,0:T(8,128)(2,1)S(1)}, bf16[192,768]{1,0:T(8,128)(2,1)}, u32[]{:S(2)}) copy-start(bf16[192,768]{1,0:T(8,128)(2,1)} %param.24) | copy-start | bytes 884740
  24.4 5.5 %copy-start.9 = (f32[2,192,768]{2,1,0:T(8,128)S(1)}, f32[2,192,768]{2,1,0:T(8,128)}, u32[]{:S(2)}) copy-start(f32[2,192,768]{2,1,0:T(8,128)} %param.27) | copy-start | bytes 3538948
  25.3 9.0 %slice-start = ((s8[4718592]{0:T(1024)(128)(4,1)}), s8[524288]{0:T(1024)(128)(4,1)S(1)}, s32[]{:S(2)}) async-start(s8[4718592]{0:T(1024)(128)(4,1)} %bitcast.100), calls=%async_computation | async-start | bytes 1048576
  28.2 3.4 copy-start.4
  31.4 2.0 copy-start.5
  31.4 3.1 slice-start.1
  472.0 2.5 copy-start.2
  482.0 5.4 %copy-start.3 = (bf16[4,4,96,384]{3,2,1,0:T(8,128)(2,1)S(1)}, bf16[4,4,96,384]{3,2,1,0:T(8,128)(2,1)}, u32[]{:S(2)}) copy-start(bf16[4,4,96,384]{3,2,1,0:T(8,128)(2,1)} %get-tuple-element.116) | copy-start | bytes 3538948
  514.7 6.2 %copy-start.6 = (f32[192,768]{1,0:T(8,128)S(1)}, f32[192,768]{1,0:T(8,128)}, u32[]{:S(2)}) copy-start(f32[192,768]{1,0:T(8,128)} %get-tuple-element.230) | copy-start | bytes 1769476
  514.7 7.0 %copy-start.1 = (f32[2,2,768,64]{2,3,1,0:T(8,128)S(1)}, f32[2,2,768,64]{2,3,1,0:T(8,128)}, u32[]{:S(2)}) copy-start(f32[2,2,768,64]{2,3,1,0:T(8,128)} %param.33) | copy-start | bytes 2359300
